TPU v7x, 128 devices: a whole 4x4x4 slice. The times are simulated.
128 devices in a mesh: seg: 4 (over x_hi, core), ch: 32 (over z, y, x_lo).
Axes of the slice: x: 4 (x_hi: 2, x_lo: 2; x = x_hi * 2 + x_lo), y: 4, z: 4, core: 2. Of those that a mesh axis runs over, the one named last changes fastest.
Arguments:
- raw: bfloat16 [64, 4096, 1024], P('seg', 'ch')
- source_index: int32 [16], replicated, may hold values from 0 to 4095, as said below
- source_block: int32 [16], replicated, may hold values from 0 to 3, as said below
Outputs:
- stacked: float32 [4096, 16, 128], P(('ch', 'seg'))
Inputs may be any that keep to these rules, and one draw needn't show every extreme that they name: `source_index`: the 16 channels are distinct. `source_block`: every block holds exactly 4 sources.
All inputs are finite; a program needn't handle non-finite values.
Results may differ from a plain program's by a relative error of at most 0.002.
Values may be sent and summed in bfloat16 or wider, within the bound.
No kernel may reach another device: no remote copies, remote signals or barrier semaphores. Data moves between devices by JAX's collectives and lax.ppermute only.
A program may use at most 64 MiB of HBM per device.

v0:
```python
import math

import jax
import jax.numpy as jnp
from jax import lax
from jax.sharding import PartitionSpec as P

HALFLAG = 64
SMOOTH = 4
SOURCES = 16
PER_BLOCK = 4


WATER = 0.1
EPS = 1e-06


def dft_table(length, count):
    times = lax.broadcasted_iota(jnp.int32, (length, count), 0)
    bins = lax.broadcasted_iota(jnp.int32, (length, count), 1) + 1
    phase = (bins * times % length).astype(jnp.float32) * (2.0 * math.pi / length)
    return jnp.concatenate([jnp.cos(phase), -jnp.sin(phase)], axis=1).astype(jnp.bfloat16)


def lag_tables(count, length, half):
    bins = lax.broadcasted_iota(jnp.int32, (count, 2 * half), 0) + 1
    shifts = lax.broadcasted_iota(jnp.int32, (count, 2 * half), 1) - half
    theta = (bins * shifts % length).astype(jnp.float32) * (2.0 * math.pi / length)
    return (jnp.cos(theta), jnp.sin(theta))


def whiten_rows(spectrum, count, half):
    real = spectrum[:, :count]
    imag = spectrum[:, count:]
    amplitude = jnp.sqrt(real * real + imag * imag)
    padded = jnp.pad(amplitude, ((0, 0), (half, half)))
    smoothed = padded[:, 0:count]
    for shift in range(1, 2 * half + 1):
        smoothed = smoothed + padded[:, shift : shift + count]
    smoothed = smoothed / (2 * half + 1)
    level = jnp.mean(amplitude, axis=1, keepdims=True)
    divisor = smoothed + WATER * level + EPS
    return (spectrum / jnp.concatenate([divisor, divisor], axis=1)).astype(jnp.bfloat16)


def slot_channels(source_index, source_block, per_block):
    count = source_index.shape[0]
    later = lax.broadcasted_iota(jnp.int32, (count, count), 0) > lax.broadcasted_iota(
        jnp.int32, (count, count), 1
    )
    same = source_block[:, None] == source_block[None, :]
    rank = jnp.sum(jnp.where(later & same, 1, 0), axis=1).astype(jnp.int32)
    slot = source_block * per_block + rank
    place = slot[None, :] == lax.broadcasted_iota(jnp.int32, (count, count), 0)
    return jnp.sum(jnp.where(place, source_index[None, :], 0), axis=1)


def build_kernel(spec, cos_table, sin_table, count):
    real = spec[:, :count][:, :, None]
    imag = spec[:, count:][:, :, None]
    real_part = real * cos_table[None] - imag * sin_table[None]
    imag_part = real * sin_table[None] + imag * cos_table[None]
    joined = jnp.concatenate([real_part, imag_part], axis=1)
    width = joined.shape[0] * joined.shape[2]
    return jnp.transpose(joined, (1, 0, 2)).reshape(2 * count, width).astype(jnp.bfloat16)


def correlate(whitened, sources, cos_table, sin_table, count, scale):

    def one_segment(total, pair):
        rows, spec = pair
        kernel = build_kernel(spec, cos_table, sin_table, count)
        term = jnp.dot(rows, kernel, preferred_element_type=jnp.float32)
        return (total + term * scale, None)

    width = sources.shape[1] * cos_table.shape[1]
    start = jnp.zeros((whitened.shape[1], width), jnp.float32)
    total, unused = lax.scan(one_segment, start, (whitened, sources))
    return total


def local(raw, source_index, source_block):
    seg_local, ch_local, length = raw.shape
    count = length // 2
    half = HALFLAG
    table = dft_table(length, count)
    cos_table, sin_table = lag_tables(count, length, half)
    spectrum = jnp.dot(
        raw.reshape(seg_local * ch_local, length), table, preferred_element_type=jnp.float32
    )
    whitened = whiten_rows(spectrum, count, SMOOTH).reshape(seg_local, ch_local, 2 * count)
    slot_channel = slot_channels(source_index, source_block, PER_BLOCK)
    first = lax.axis_index("ch") * ch_local
    local_rows = first + lax.broadcasted_iota(jnp.int32, (SOURCES, ch_local), 1)
    select = (slot_channel[:, None] == local_rows).astype(jnp.bfloat16)
    local_spec = jnp.einsum("qr,grk->gqk", select, whitened, preferred_element_type=jnp.float32)
    scale = 1.0 / (count * seg_local * lax.axis_size("seg"))
    source_spec = lax.psum(local_spec.astype(jnp.bfloat16), "ch").astype(jnp.float32)
    term = correlate(whitened, source_spec, cos_table, sin_table, count, scale)
    term = term.reshape(ch_local, SOURCES, 2 * half)
    share = ch_local // lax.axis_size("seg")
    summed = lax.psum(term, "seg")
    return lax.dynamic_slice_in_dim(summed, lax.axis_index("seg") * share, share, 0)


def solution(mesh):
    return jax.shard_map(
        local,
        mesh=mesh,
        in_specs=(P("seg", "ch", None), P(), P()),
        out_specs=P(("ch", "seg"), None, None),
        check_vma=False,
    )
```

profile of v0, /device:TPU:1, one launch (start us, length us, event | category | flops | bytes accessed | tf_op | source)
XLA Modules:
  0.0 586.8 jit_solution(4811285551378488082)
XLA Ops:
  6.5 8.6 %cosine_convert_fusion = (bf16[1024,512]{1,0:T(8,128)(2,1)S(1)}, bf16[1024,512]{1,0:T(8,128)(2,1)S(1)}) fusion(s32[512]{0:T(512)S(1)} %iota_add_fusion), kind=kLoop, calls=%fused_computation.46 | loop fusion | flops 8912896 | bytes 2099200 | tf_op jit(solution)/shard_map/convert.2
  15.2 6.4 %convolution_bitcast_fusion = f32[2048,1024]{0,1:T(8,128)S(1)} fusion(bf16[2048,1024]{1,0:T(8,128)(2,1)} %bitcast.39, bf16[1024,512]{1,0:T(8,128)(2,1)S(1)} %get-tuple-element.175, bf16[1024,512]{1,0:T(8,128)(2,1)S(1)} %get-tuple-element.174), kind=kOutput, calls=%fused_computation.23 | convolution fusion | flops 4299161600 | bytes 14680064 | tf_op jit(solution)/shard_map/dot_general | solution.py:88
  23.2 5.0 add_add_fusion
  28.2 4.5 fusion.18
  32.7 3.4 copy.10
  36.4 5.5 convert_bitcast_fusion
  42.1 6.7 %copy.8 = bf16[16,128,1024]{2,1,0:T(8,128)(2,1)} copy(bf16[16,128,1024]{1,0,2:T(8,128)(2,1)} %bitcast.36) | data formatting | bytes 8388608
  48.9 313.4 %all-reduce.4.cloned.1.call-done = bf16[16,16,1024]{1,0,2:T(8,128)(2,1)} async-done(((bf16[16,16,1024]{1,0,2:T(8,128)(2,1)}), bf16[16,16,1024]{1,0,2:T(8,128)(2,1)}) %all-reduce.4.cloned.1.call-update) | async-done | bytes 524304 | tf_op jit(solution)/shard_map/psum | solution.py:98
  362.3 4.6 copy.9
  366.9 144.2 %while.14 = (s32[]{:T(128)}, f32[128,2048]{1,0:T(8,128)S(1)}, bf16[16,128,1024]{2,1,0:T(8,128)(2,1)}, f32[16,16,1024]{2,1,0:T(8,128)S(1)}, s32[128]{0:T(128)S(1)}, /*index=5*/s32[512]{0:T(512)S(1)}, s32[]{:T(128)}, s32[]{:T(128)}) while((s32[]{:T(128)}, f32[128,2048]{1,0:T(8,128)S(1)}, ...), condition=%wide.region_5.6_spmd.clone.clone.clone.clone, body=%wide.region_4.5_spmd.clone.clone.clone.clone.sunk | while | flops 555352064 | bytes 20515940 | solution.py:78
  371.9 4.0 fusion.49
  381.0 4.0 fusion.49
  387.4 2.5 pad_maximum_fusion.2
  390.0 4.0 fusion.49
  399.0 4.0 fusion.49
  408.0 4.0 fusion.49
  414.5 2.5 pad_maximum_fusion.2
  417.0 4.0 fusion.49
  426.0 4.0 fusion.49
  435.0 4.0 fusion.49
  441.5 2.5 pad_maximum_fusion.2
  444.0 4.0 fusion.49
  453.0 4.0 fusion.49
  462.0 4.0 fusion.49
  468.5 2.5 pad_maximum_fusion.2
  471.1 4.0 fusion.49
  480.1 4.0 fusion.49
  489.1 4.0 fusion.49
  495.6 2.5 pad_maximum_fusion.2
  498.1 4.0 fusion.49
  507.1 4.0 fusion.49
  512.3 66.0 %all-reduce.6.cloned.1.call-done = f32[128,16,128]{2,1,0:T(8,128)} async-done(((f32[128,16,128]{2,1,0:T(8,128)}), f32[128,16,128]{2,1,0:T(8,128)}) %all-reduce.6.cloned.1.call-update) | async-done | bytes 1048592 | tf_op jit(solution)/shard_map/psum | solution.py:102
  (94 shorter events, 72.1 us)
Async XLA Ops:
  6.5 355.7 %all-reduce.4.cloned.1.call-start = ((), (), s32[]{:S(2)}) async-start(), calls=%async_computation | async-start | bytes 8388608 | tf_op jit(solution)/shard_map/psum | solution.py:98
  32.7 3.4 copy-start
  32.7 3.6 copy-start.1
  41.9 536.4 %all-reduce.6.cloned.1.call-start = ((), (), s32[]{:S(2)}) async-start(), calls=%async_computation.1 | async-start | bytes 2097152 | tf_op jit(solution)/shard_map/psum | solution.py:102
Sparse Core Ops, SparseCore 0:
  42.0 320.2 all-reduce.3
  512.5 65.7 all-reduce.5
where the time goes:
time: 587 us
  waiting for transfers between devices  379 us (65%)
  other arithmetic  99.5 us (17%)
  matrix products  75.5 us (13%)
  local copies, waits for them, and re-layouts  17.9 us (3%)
  between operations  13.5 us (2%)
    psum x1, waiting for transfers between devices, local(): lax.psum(local_spec.astype(jnp.bfloat16), 'ch').astype(jnp.float32)  313 us
    psum x1, waiting for transfers between devices, local(): summed = lax.psum(term, 'seg')  66 us
    dot_general x16, matrix products, one_segment(): term = jnp.dot(rows, kernel, preferred_element_type=jnp.float32)  63.6 us
    concatenate x16, other arithmetic, build_kernel(): joined = jnp.concatenate([real_part, imag_part], axis=1)  40.4 us
    another operation x17, other arithmetic  30.1 us
    cos x16, other arithmetic, lag_tables(): return (jnp.cos(theta), jnp.sin(theta))  17.6 us
    unnamed x8, local copies, waits for them, and re-layouts  16 us
  transfers between devices with their start and end apart: 2, of which 2 were waited for; matrix products, arithmetic and copies ran while one was open for 1% of the time, Pallas kernels for 0%

commit v1 on v0

v1 whole, which is shorter than its diff:
```python
import jax
import jax.numpy as jnp
import ml_dtypes
import numpy as np
from jax import lax
from jax.experimental import pallas as pl
from jax.experimental.pallas import tpu as pltpu
from jax.sharding import PartitionSpec as P

SEGLEN = 1024
FREQS = 512
HALFLAG = 64
LAGS = 128
SMOOTH = 4
SOURCES = 16
PER_BLOCK = 4
WATER = 0.1
EPS = 1e-06

GROUPS = FREQS // 8
MIB = 1 << 20


def dft_rows():
    bins = np.arange(1, FREQS + 1)[:, None]
    times = np.arange(SEGLEN)[None, :]
    phase = ((bins * times) % SEGLEN).astype(np.float32) * np.float32(2.0 * np.pi / SEGLEN)
    table = np.concatenate([np.cos(phase), -np.sin(phase)], axis=0)
    return table.astype(ml_dtypes.bfloat16)


def lag_rows(scale):
    bins = np.arange(1, FREQS + 1)[None, :]
    lags = np.arange(LAGS)[:, None] - HALFLAG
    theta = ((bins * lags) % SEGLEN).astype(np.float32) * np.float32(2.0 * np.pi / SEGLEN)
    cos = np.cos(theta).reshape(LAGS, GROUPS, 1, 8)
    sin = np.sin(theta).reshape(LAGS, GROUPS, 1, 8)
    table = np.concatenate([cos, sin], axis=2).reshape(LAGS, 2 * FREQS) * np.float32(scale)
    high = table.astype(ml_dtypes.bfloat16)
    low = (table - high.astype(np.float32)).astype(ml_dtypes.bfloat16)
    return np.concatenate([high, low], axis=0)


def nt_dot(a, b):
    return lax.dot_general(a, b, (((1,), (1,)), ((), ())), preferred_element_type=jnp.float32)


def nn_dot(a, b):
    return lax.dot_general(a, b, (((1,), (0,)), ((), ())), preferred_element_type=jnp.float32)


def pick_body(index_ref, block_ref, raw_ref, out_ref, chan_ref, sel_ref):
    count = raw_ref.shape[1]

    @pl.when(pl.program_id(0) == 0)
    def _():
        first = lax.axis_index("ch") * count
        for s in range(SOURCES):
            rank = jnp.int32(0)
            for t in range(s):
                rank += jnp.where(block_ref[t] == block_ref[s], 1, 0).astype(jnp.int32)
            chan_ref[block_ref[s] * PER_BLOCK + rank] = index_ref[s] - first
        lane = lax.broadcasted_iota(jnp.int32, (8, count), 1)
        sub = lax.broadcasted_iota(jnp.int32, (8, count), 0)
        for q in range(SOURCES):
            hit = jnp.where(lane == chan_ref[q], 1.0, 0.0)
            for g in range(8):
                sel_ref[q * 8 : q * 8 + 8, g * count : (g + 1) * count] = jnp.where(sub == g, hit, 0.0)

    rows = raw_ref[...].reshape(8 * count, SEGLEN)
    got = nn_dot(sel_ref[...].astype(jnp.bfloat16), rows)
    out_ref[...] = got.astype(jnp.bfloat16).reshape(SOURCES, 1, 8, SEGLEN)


def pick(raw, source_index, source_block):
    segs, count, length = raw.shape
    return pl.pallas_call(
        pick_body,
        grid=(segs // 8,),
        in_specs=[
            pl.BlockSpec(memory_space=pltpu.SMEM),
            pl.BlockSpec(memory_space=pltpu.SMEM),
            pl.BlockSpec((8, count, length), lambda i: (i, 0, 0)),
        ],
        out_specs=pl.BlockSpec((SOURCES, 1, 8, length), lambda i: (0, i, 0, 0)),
        out_shape=jax.ShapeDtypeStruct((SOURCES, segs // 8, 8, length), jnp.bfloat16),
        scratch_shapes=[
            pltpu.SMEM((SOURCES,), jnp.int32),
            pltpu.VMEM((SOURCES * 8, 8 * count), jnp.float32),
        ],
        compiler_params=pltpu.CompilerParams(vmem_limit_bytes=32 * MIB),
        cost_estimate=pl.CostEstimate(flops=2 * 10**8, bytes_accessed=5 * 10**6, transcendentals=0),
        name="pick",
    )(source_index, source_block, raw)


def source_body(parts_ref, table_ref, out_ref):
    total = jnp.sum(parts_ref[...].astype(jnp.float32), axis=0)
    spectrum = nt_dot(total.astype(jnp.bfloat16), table_ref[...])
    real = spectrum[:, :FREQS]
    imag = spectrum[:, FREQS:]
    amplitude = jnp.sqrt(real * real + imag * imag)
    place = lax.broadcasted_iota(jnp.int32, amplitude.shape, 1)
    smoothed = amplitude
    for shift in range(1, SMOOTH + 1):
        later = pltpu.roll(amplitude, FREQS - shift, 1)
        smoothed += jnp.where(place < FREQS - shift, later, 0.0)
        earlier = pltpu.roll(amplitude, shift, 1)
        smoothed += jnp.where(place >= shift, earlier, 0.0)
    level = jnp.sum(amplitude, axis=1, keepdims=True) * (1.0 / FREQS)
    divisor = smoothed / (2 * SMOOTH + 1) + WATER * level + EPS
    real = (real / divisor).astype(jnp.bfloat16).astype(jnp.float32)
    imag = (imag / divisor).astype(jnp.bfloat16).astype(jnp.float32)
    sub = lax.broadcasted_iota(jnp.int32, (8, 128), 0)
    lane = lax.broadcasted_iota(jnp.int32, (8, 128), 1)
    block = (lane // 8) % 8

    def turn(x):
        for s in (4, 2, 1):
            down = pltpu.roll(pltpu.roll(x, s, 0), 128 - 8 * s, 1)
            up = pltpu.roll(pltpu.roll(x, 8 - s, 0), 8 * s, 1)
            low_row = (sub & s) == 0
            low_block = (block & s) == 0
            x = jnp.where(low_row == low_block, x, jnp.where(low_row, up, down))
        return x

    rows = []
    for j in range(FREQS // 128):
        re = turn(real[:, j * 128 : (j + 1) * 128])
        im = turn(imag[:, j * 128 : (j + 1) * 128])
        rows.append(jnp.where(lane < 64, re, pltpu.roll(im, 64, 1)))
        rows.append(jnp.where(lane < 64, pltpu.roll(re, 64, 1), im))
    packed = jnp.concatenate(rows, axis=0).astype(jnp.bfloat16)
    out_ref[...] = jnp.broadcast_to(packed[None], out_ref.shape)


def source_rows(parts, table):
    return pl.pallas_call(
        source_body,
        out_shape=jax.ShapeDtypeStruct((parts.shape[0], GROUPS, 128), jnp.bfloat16),
        in_specs=[pl.BlockSpec(memory_space=pltpu.VMEM)] * 2,
        out_specs=pl.BlockSpec(memory_space=pltpu.VMEM),
        compiler_params=pltpu.CompilerParams(vmem_limit_bytes=32 * MIB),
        cost_estimate=pl.CostEstimate(flops=2 * 8 * 1024 * 1024, bytes_accessed=3 * 10**6, transcendentals=0),
        name="source_rows",
    )(parts, table)


def whiten_body(raw_ref, table_ref, out_ref, spec_ref, amp_ref):
    width = raw_ref.shape[0] * raw_ref.shape[1]
    count = raw_ref.shape[1]
    rows = raw_ref[...].reshape(width, SEGLEN)
    spec_ref[...] = nt_dot(table_ref[...], rows)
    zero = jnp.zeros((8, width), jnp.float32)
    amp_ref[0:8, :] = zero
    amp_ref[FREQS + 8 : FREQS + 16, :] = zero
    step = 32
    level = zero
    for f in range(0, FREQS, step):
        real = spec_ref[f : f + step, :]
        imag = spec_ref[FREQS + f : FREQS + f + step, :]
        amplitude = jnp.sqrt(real * real + imag * imag)
        amp_ref[8 + f : 8 + f + step, :] = amplitude
        for i in range(0, step, 8):
            level += amplitude[i : i + 8]
    level = jnp.sum(level, axis=0, keepdims=True) * (WATER / FREQS) + EPS
    for f in range(0, FREQS, step):
        size = step + 16
        a = amp_ref[f : f + size, :]
        s2 = a + pltpu.roll(a, size - 1, 0)
        s4 = s2 + pltpu.roll(s2, size - 2, 0)
        s9 = s4 + pltpu.roll(s4, 4, 0) + pltpu.roll(a, size - 4, 0)
        inverse = 1.0 / (s9[8 : 8 + step] * (1.0 / (2 * SMOOTH + 1)) + level)
        real = spec_ref[f : f + step, :] * inverse
        imag = spec_ref[FREQS + f : FREQS + f + step, :] * inverse
        for part, value in ((0, real), (1, imag)):
            for i in range(0, step, 8):
                pair = jnp.concatenate(
                    [value[i : i + 8, :count], value[i : i + 8, count:]], axis=0
                )
                out_ref[(f + i) // 8, part, 0] = pair.astype(jnp.bfloat16)


def whiten(raw, table, half):
    segs, count, length = raw.shape
    pairs = segs // 4
    out = pl.pallas_call(
        whiten_body,
        grid=(pairs,),
        in_specs=[
            pl.BlockSpec((2, count, length), lambda i: (i + half * pairs, 0, 0)),
            pl.BlockSpec((2 * FREQS, length), lambda i: (0, 0)),
        ],
        out_specs=pl.BlockSpec((GROUPS, 2, 1, 16, count), lambda i: (0, 0, i, 0, 0)),
        out_shape=jax.ShapeDtypeStruct((GROUPS, 2, pairs, 16, count), jnp.bfloat16),
        scratch_shapes=[
            pltpu.VMEM((2 * FREQS, 2 * count), jnp.float32),
            pltpu.VMEM((FREQS + 16, 2 * count), jnp.float32),
        ],
        compiler_params=pltpu.CompilerParams(vmem_limit_bytes=32 * MIB),
        cost_estimate=pl.CostEstimate(
            flops=2 * 1024 * 1024 * 1024, bytes_accessed=6 * 10**6, transcendentals=10**6
        ),
        name=f"whiten{half}",
    )(raw, table)
    return out.reshape(GROUPS, 32 * pairs, count)


def correlate_body(src_ref, w0_ref, w1_ref, lag_ref, mine_ref, core_ref, far0_ref, far1_ref, s_ref, high_ref, low_ref, sum_ref):
    step = pl.program_id(0)
    blocks = w0_ref.shape[0]
    count = w0_ref.shape[2]
    pairs = SOURCES // 2

    @pl.when(step == 0)
    def _():
        lane = lax.broadcasted_iota(jnp.int32, (GROUPS, 128), 1)
        for i in range(2 * SOURCES):
            value = src_ref[i].astype(jnp.float32)
            s_ref[0, i] = value
            turned = pltpu.roll(value, 64, 1)
            s_ref[1, i] = jnp.where(lane < 64, -turned, turned)

    sub = lax.broadcasted_iota(jnp.int32, (8, 128), 0)
    lane = lax.broadcasted_iota(jnp.int32, (8, 128), 1)
    diagonal = (lane % 8) == sub
    for j in range(blocks):
        b = step * blocks + j
        tiles = []
        for q in range(SOURCES):
            halves = []
            for h in range(2):
                parts = []
                for r in range(2):
                    row = jnp.broadcast_to(s_ref[r, 2 * q + h, pl.ds(b, 1), :], (8, 128))
                    parts.append(jnp.where(diagonal, row, 0.0))
                halves.append(jnp.concatenate(parts, axis=0).astype(jnp.bfloat16))
            tiles.append(jnp.concatenate(halves, axis=1))
        left = jnp.concatenate(tiles, axis=0)
        right = jnp.concatenate([w0_ref[j], w1_ref[j]], axis=0)
        cross = nn_dot(left, right)
        high = cross.astype(jnp.bfloat16)
        low = (cross - high.astype(jnp.float32)).astype(jnp.bfloat16)
        at = pl.ds(pl.multiple_of(b * 16, 16), 16)
        for q in range(SOURCES):
            cols = slice((q % 2) * count, (q % 2 + 1) * count)
            high_ref[q // 2, at, cols] = high[q * 16 : q * 16 + 16]
            low_ref[q // 2, at, cols] = low[q * 16 : q * 16 + 16]

    @pl.when(step == pl.num_programs(0) - 1)
    def _():
        me = lax.axis_index("seg")
        share = count // 4
        for p in range(pairs):
            first = nn_dot(lag_ref[...], high_ref[p])
            second = nn_dot(lag_ref[:LAGS, :], low_ref[p])
            total = first[:LAGS] + (first[LAGS:] + second)
            for i in range(2):
                sum_ref[2 * p + i] = total[:, i * count : (i + 1) * count].T

        def part(r):
            return sum_ref[:, pl.ds(pl.multiple_of((me ^ r) * share, share), share), :]

        mine_ref[...] = part(0)
        core_ref[...] = part(1)
        far0_ref[...] = part(2).astype(jnp.bfloat16)
        far1_ref[...] = part(3).astype(jnp.bfloat16)


def correlate(src, w0, w1, lag):
    count = w0.shape[2]
    blocks = 8
    share = count // 4
    shape = (SOURCES, share, LAGS)
    whole = pl.BlockSpec(shape, lambda i: (0, 0, 0))
    return pl.pallas_call(
        correlate_body,
        grid=(GROUPS // blocks,),
        in_specs=[
            pl.BlockSpec(src.shape, lambda i: (0, 0, 0)),
            pl.BlockSpec((blocks, 128, count), lambda i: (i, 0, 0)),
            pl.BlockSpec((blocks, 128, count), lambda i: (i, 0, 0)),
            pl.BlockSpec(lag.shape, lambda i: (0, 0)),
        ],
        out_specs=[whole] * 4,
        out_shape=[
            jax.ShapeDtypeStruct(shape, jnp.float32),
            jax.ShapeDtypeStruct(shape, jnp.float32),
            jax.ShapeDtypeStruct(shape, jnp.bfloat16),
            jax.ShapeDtypeStruct(shape, jnp.bfloat16),
        ],
        scratch_shapes=[
            pltpu.VMEM((2, 2 * SOURCES, GROUPS, 128), jnp.float32),
            pltpu.VMEM((SOURCES // 2, 2 * FREQS, 2 * count), jnp.bfloat16),
            pltpu.VMEM((SOURCES // 2, 2 * FREQS, 2 * count), jnp.bfloat16),
            pltpu.VMEM((SOURCES, count, LAGS), jnp.float32),
        ],
        compiler_params=pltpu.CompilerParams(vmem_limit_bytes=40 * MIB),
        cost_estimate=pl.CostEstimate(flops=3 * 10**9, bytes_accessed=6 * 10**6, transcendentals=0),
        name="correlate",
    )(src, w0, w1, lag)


def gather_sum_body(mine_ref, core_ref, far0_ref, far1_ref, out_ref):
    far = far0_ref[...].astype(jnp.float32) + far1_ref[...].astype(jnp.float32)
    total = (mine_ref[...] + core_ref[...]) + far
    for q in range(SOURCES):
        out_ref[:, q, :] = total[q]


def gather_sum(mine, core, far0, far1):
    shape = mine.shape
    return pl.pallas_call(
        gather_sum_body,
        in_specs=[pl.BlockSpec(memory_space=pltpu.VMEM)] * 4,
        out_specs=pl.BlockSpec(memory_space=pltpu.VMEM),
        out_shape=jax.ShapeDtypeStruct((shape[1], shape[0], shape[2]), jnp.float32),
        cost_estimate=pl.CostEstimate(flops=10**6, bytes_accessed=10**6, transcendentals=0),
        name="gather_sum",
    )(mine, core, far0, far1)


def local(raw, source_index, source_block):
    segs = raw.shape[0] * lax.axis_size("seg")
    ways = lax.axis_size("ch")
    table = jnp.asarray(dft_rows())
    lag = jnp.asarray(lag_rows(1.0 / (FREQS * segs)))
    picked = pick(raw, source_index, source_block).reshape(ways, 8, SEGLEN)
    parts = lax.all_to_all(picked, "ch", 0, 0)
    w0 = whiten(raw, table, 0)
    spread = source_rows(parts, table)
    src = lax.all_to_all(spread, "ch", 0, 0)
    w1 = whiten(raw, table, 1)
    mine, core, far0, far1 = correlate(src, w0, w1, lag)

    def swap(x, r):
        return lax.ppermute(x, "seg", [(i, i ^ r) for i in range(4)])

    return gather_sum(mine, swap(core, 1), swap(far0, 2), swap(far1, 3))


def solution(mesh):
    return jax.shard_map(
        local,
        mesh=mesh,
        in_specs=(P("seg", "ch", None), P(), P()),
        out_specs=P(("ch", "seg"), None, None),
        check_vma=False,
    )
```

time: 587 us -> 71.6 us (0.12)
  waiting for transfers between devices: 379 us -> 6.5 us
  other arithmetic: 99.5 us -> 0 us
  matrix products: 75.5 us -> 0 us
  Pallas kernels: 0 us -> 21.8 us
  blocking collectives: 0 us -> 20.7 us
  between operations: 13.5 us -> 0.09 us
  starting transfers between devices: 0.22 us -> 9.15 us
    psum x2 -> x0, waiting for transfers between devices: 379 us -> none  [the longest x1 313 us: local(): lax.psum(local_spec.astype(jnp.bfloat16), 'ch').astype(jnp.float32)]
    dot_general x18 -> x0, matrix products: 75.5 us -> none  [the longest x16 63.6 us: one_segment(): term = jnp.dot(rows, kernel, preferred_element_type=jnp.float32)]
    concatenate x16 -> x0, other arithmetic: 40.4 us -> none  [build_kernel(): joined = jnp.concatenate([real_part, imag_part], axis=1)]
    another operation x17 -> x0, other arithmetic: 30.1 us -> none
    pallas_call x0 -> x6, Pallas kernels: none -> 21.8 us  [the longest x2 9.98 us: whiten(): pl.pallas_call(whiten_body, grid=(pairs,), in_specs=[pl.BlockSpec((2, cou...]
    all_to_all x0 -> x1, blocking collectives: none -> 20.7 us  [local(): parts = lax.all_to_all(picked, 'ch', 0, 0)]
    cos x16 -> x0, other arithmetic: 17.6 us -> none  [lag_tables(): return (jnp.cos(theta), jnp.sin(theta))]
    ppermute x0 -> x3, waiting for transfers between devices: none -> 6.49 us  [swap(): return lax.ppermute(x, 'seg', [(i, i ^ r) for i in range(4)])]
  transfers between devices with their start and end apart: 2 -> 4, of which waited for: 2 -> 2; matrix products, arithmetic and copies ran while one was open for 1% -> 0% of each run, Pallas kernels for 0% -> 14%
where the time goes in v1:
time: 71.6 us; the launch traced here: 71.2 us
  Pallas kernels  21.8 us (30%)
  blocking collectives  20.7 us (29%)
  local copies, waits for them, and re-layouts  12.9 us (18%)
  starting transfers between devices  9.15 us (13%)
  waiting for transfers between devices  6.5 us (9%)
    all_to_all x1, blocking collectives, local(): parts = lax.all_to_all(picked, 'ch', 0, 0)  20.7 us
    unnamed x28, local copies, waits for them, and re-layouts  12.9 us
    pallas_call x2, Pallas kernels, whiten(): pl.pallas_call(whiten_body, grid=(pairs,), in_specs=[pl.BlockSpec((2, cou...  9.98 us
    ppermute x3, waiting for transfers between devices, swap(): return lax.ppermute(x, 'seg', [(i, i ^ r) for i in range(4)])  6.49 us
    pallas_call x1, Pallas kernels, correlate(): pl.pallas_call(correlate_body, grid=(GROUPS // blocks,), in_specs=[pl.Blo...  6.18 us
    ppermute x3, starting transfers between devices, swap(): return lax.ppermute(x, 'seg', [(i, i ^ r) for i in range(4)])  5.26 us
    all_to_all x1, starting transfers between devices, local(): src = lax.all_to_all(spread, 'ch', 0, 0)  3.89 us
    pallas_call x1, Pallas kernels, gather_sum(): pl.pallas_call(gather_sum_body, in_specs=[pl.BlockSpec(memory_space=pltpu...  1.97 us
  transfers between devices with their start and end apart: 4, of which 2 were waited for; matrix products, arithmetic and copies ran while one was open for 0% of the time, Pallas kernels for 14%

profile of v1, /device:TPU:1, one launch (start us, length us, event | category | flops | bytes accessed | tf_op | source)
XLA Modules:
  0.0 71.2 jit_solution(5930256047961986423)
XLA Ops:
  0.0 2.2 %copy-done = bf16[16,128,1024]{2,1,0:T(8,128)(2,1)S(1)} copy-done((bf16[16,128,1024]{2,1,0:T(8,128)(2,1)S(1)}, bf16[16,128,1024]{2,1,0:T(8,128)(2,1)}, u32[]{:S(2)}) %copy-start) | copy-done | bytes 4194328
  2.2 0.7 copy-done.8
  2.8 0.7 copy-done.9
  3.5 1.7 %pick.1 = bf16[16,2,8,1024]{3,2,1,0:T(8,128)(2,1)S(1)} custom-call(s32[16]{0:T(128)S(1)} %copy-done.8, s32[16]{0:T(128)S(1)} %copy-done.9, bf16[16,128,1024]{2,1,0:T(8,128)(2,1)S(1)} %copy-done), custom_call_target="tpu_custom_call" | custom-call | flops 200000000 | bytes 5000000 | tf_op jit(solution)/shard_map/pick/pallas_call | solution.py:77
  5.3 20.7 %all_to_all.10.parts_ref = bf16[32,8,1024]{2,1,0:T(8,128)(2,1)S(1)} all-to-all(bf16[32,8,1024]{2,1,0:T(8,128)(2,1)S(1)} %bitcast.3), channel_id=1, replica_groups=mesh['seg'=4,'ch'=32] {'ch'}, dimensions={0} | all-to-all | bytes 1048576 | tf_op jit(solution)/shard_map/all_to_all | solution.py:329
  26.0 0.0 copy-done.2
  26.0 1.9 %source_rows.1 = bf16[32,64,128]{2,1,0:T(8,128)(2,1)} custom-call(bf16[32,8,1024]{2,1,0:T(8,128)(2,1)S(1)} %all_to_all.10.parts_ref, bf16[1024,1024]{1,0:T(8,128)(2,1)S(1)} %copy-done.2), custom_call_target="tpu_custom_call" | custom-call | flops 16777216 | bytes 3000000 | tf_op jit(solution)/shard_map/source_rows/pallas_call | solution.py:138
  27.9 3.9 %all-to-all-start.1 = ((bf16[32,64,128]{2,1,0:T(8,128)(2,1)}), bf16[32,64,128]{2,1,0:T(8,128)(2,1)S(1)}, u32[]{:S(2)}, u32[]{:S(2)}) async-start(bf16[32,64,128]{2,1,0:T(8,128)(2,1)} %source_rows.1), calls=%async_computation.1 | async-start | bytes 1048576 | tf_op jit(solution)/shard_map/all_to_all | solution.py:332
  31.8 0.0 copy-start.1
  31.8 2.2 %copy-done.1 = bf16[16,128,1024]{2,1,0:T(8,128)(2,1)S(1)} copy-done((bf16[16,128,1024]{2,1,0:T(8,128)(2,1)S(1)}, bf16[16,128,1024]{2,1,0:T(8,128)(2,1)}, u32[]{:S(2)}) %copy-start.1) | copy-done | bytes 4194328
  34.0 5.0 %whiten1.1 = bf16[64,2,4,16,128]{4,3,2,1,0:T(8,128)(2,1)S(1)} custom-call(bf16[16,128,1024]{2,1,0:T(8,128)(2,1)S(1)} %copy-done.1, bf16[1024,1024]{1,0:T(8,128)(2,1)S(1)} %copy-done.2), custom_call_target="tpu_custom_call" | custom-call | flops 2147483648 | bytes 6000000 | tf_op jit(solution)/shard_map/whiten1/pallas_call | solution.py:187
  39.0 0.0 copy-start.3
  39.0 1.3 %copy-done.3 = bf16[64,2,4,16,128]{4,3,2,1,0:T(8,128)(2,1)} copy-done((bf16[64,2,4,16,128]{4,3,2,1,0:T(8,128)(2,1)}, bf16[64,2,4,16,128]{4,3,2,1,0:T(8,128)(2,1)S(1)}, u32[]{:S(2)}) %copy-start.3) | copy-done | bytes 2097176
  40.3 5.0 %whiten0.1 = bf16[64,2,4,16,128]{4,3,2,1,0:T(8,128)(2,1)S(1)} custom-call(bf16[16,128,1024]{2,1,0:T(8,128)(2,1)S(1)} %copy-done.1, bf16[1024,1024]{1,0:T(8,128)(2,1)S(1)} %copy-done.2), custom_call_target="tpu_custom_call" | custom-call | flops 2147483648 | bytes 6000000 | tf_op jit(solution)/shard_map/whiten0/pallas_call | solution.py:187
  45.3 1.3 %copy-done.5 = bf16[64,2,4,16,128]{4,3,2,1,0:T(8,128)(2,1)} copy-done((bf16[64,2,4,16,128]{4,3,2,1,0:T(8,128)(2,1)}, bf16[64,2,4,16,128]{4,3,2,1,0:T(8,128)(2,1)S(1)}, u32[]{:S(2)}) %copy-start.5) | copy-done | bytes 2097176
  46.6 0.0 all-to-all-done.1.src_ref
  46.7 0.0 copy-done.10
  46.7 1.6 %copy-done.4 = bf16[64,2,4,16,128]{4,3,2,1,0:T(8,128)(2,1)S(1)} copy-done((bf16[64,2,4,16,128]{4,3,2,1,0:T(8,128)(2,1)S(1)}, bf16[64,2,4,16,128]{4,3,2,1,0:T(8,128)(2,1)}, u32[]{:S(2)}) %copy-start.4) | copy-done | bytes 2097176
  48.2 1.6 %copy-done.6 = bf16[64,2,4,16,128]{4,3,2,1,0:T(8,128)(2,1)S(1)} copy-done((bf16[64,2,4,16,128]{4,3,2,1,0:T(8,128)(2,1)S(1)}, bf16[64,2,4,16,128]{4,3,2,1,0:T(8,128)(2,1)}, u32[]{:S(2)}) %copy-start.6) | copy-done | bytes 2097176
  49.8 6.2 %correlate.1 = (f32[16,32,128]{2,1,0:T(8,128)S(1)}, f32[16,32,128]{2,1,0:T(8,128)S(1)}, bf16[16,32,128]{2,1,0:T(8,128)(2,1)S(1)}, bf16[16,32,128]{2,1,0:T(8,128)(2,1)S(1)}) custom-call(bf16[32,64,128]{2,1,0:T(8,128)(2,1)S(1)} %all-to-all-done.1.src_ref, bf16[64,128,128]{2,1,0:T(8,128)(2,1)S(1)} %bitcast.5, bf16[64,128,128]{2,1,0:T(8,128)(2,1)S(1)} %bitcast.4, ...), custom_call_target="tpu_custom_call" | custom-call | flops 3000000000 | bytes 6000000 | tf_op jit(solution)/shard_map/correlate/pallas_call | solution.py:276
  56.0 0.0 copy-start.7
  56.0 0.7 copy-done.7
  56.7 2.1 %collective-permute-start = (f32[16,32,128]{2,1,0:T(8,128)S(1)}, f32[16,32,128]{2,1,0:T(8,128)S(1)}, u32[]{:S(2)}, u32[]{:S(2)}) collective-permute-start(f32[16,32,128]{2,1,0:T(8,128)S(1)} %get-tuple-element.10), channel_id=1, source_target_pairs={{0,32},{32,0},{64,96},{96,64},{1,33},{33,1},{65,97},{97,65},{2,34}... | collective-permute-start | bytes 786440 | tf_op jit(solution)/shard_map/ppermute | solution.py:337
  58.8 2.4 %collective-permute-start.1 = (bf16[16,32,128]{2,1,0:T(8,128)(2,1)S(1)}, bf16[16,32,128]{2,1,0:T(8,128)(2,1)S(1)}, u32[]{:S(2)}, u32[]{:S(2)}) collective-permute-start(bf16[16,32,128]{2,1,0:T(8,128)(2,1)S(1)} %get-tuple-element.11), channel_id=1, source_target_pairs={{0,64},{32,96},{64,0},{96,32},{1,65},{33,97},{65,1},{97,33},{2,66}... | collective-permute-start | bytes 393224 | tf_op jit(solution)/shard_map/ppermute | solution.py:337
  61.3 0.7 collective-permute-start.2
  62.0 3.5 %collective-permute-done.1.far0_ref = bf16[16,32,128]{2,1,0:T(8,128)(2,1)S(1)} collective-permute-done((bf16[16,32,128]{2,1,0:T(8,128)(2,1)S(1)}, bf16[16,32,128]{2,1,0:T(8,128)(2,1)S(1)}, u32[]{:S(2)}, u32[]{:S(2)}) %collective-permute-start.1) | collective-permute-done | bytes 131104 | tf_op jit(solution)/shard_map/ppermute | solution.py:337
  65.5 3.0 %collective-permute-done.2.far1_ref = bf16[16,32,128]{2,1,0:T(8,128)(2,1)S(1)} collective-permute-done((bf16[16,32,128]{2,1,0:T(8,128)(2,1)S(1)}, bf16[16,32,128]{2,1,0:T(8,128)(2,1)S(1)}, u32[]{:S(2)}, u32[]{:S(2)}) %collective-permute-start.2) | collective-permute-done | bytes 131104 | tf_op jit(solution)/shard_map/ppermute | solution.py:337
  68.5 0.0 collective-permute-done.core_ref
  68.5 0.0 copy-done.12
  68.5 0.6 copy-done.13
  69.1 0.1 copy-done.11
  69.2 2.0 %gather_sum.1 = f32[32,16,128]{2,1,0:T(8,128)} custom-call(f32[16,32,128]{2,1,0:T(8,128)} %copy-done.7, f32[16,32,128]{2,1,0:T(8,128)} %copy-done.11, bf16[16,32,128]{2,1,0:T(8,128)(2,1)} %copy-done.12, bf16[16,32,128]{2,1,0:T(8,128)(2,1)} %copy-done.13), custom_call_target="tpu_custom_call" | custom-call | flops 1000000 | bytes 1000000 | tf_op jit(solution)/shard_map/gather_sum/pallas_call | solution.py:313
  (11 shorter events, 0.0 us)
Async XLA Ops:
  0.0 2.2 %copy-start = (bf16[16,128,1024]{2,1,0:T(8,128)(2,1)S(1)}, bf16[16,128,1024]{2,1,0:T(8,128)(2,1)}, u32[]{:S(2)}) copy-start(bf16[16,128,1024]{2,1,0:T(8,128)(2,1)} %raw_ref.5) | copy-start | bytes 12582916
  2.2 0.7 copy-start.8
  2.8 0.7 copy-start.9
  3.5 22.5 %copy-start.2 = (bf16[1024,1024]{1,0:T(8,128)(2,1)S(1)}, bf16[1024,1024]{1,0:T(8,128)(2,1)}, u32[]{:S(2)}) copy-start(bf16[1024,1024]{1,0:T(8,128)(2,1)} %constant.4.clone.table_ref) | copy-start | bytes 6291460
  27.9 18.7 %all-to-all-start.1 = ((bf16[32,64,128]{2,1,0:T(8,128)(2,1)}), bf16[32,64,128]{2,1,0:T(8,128)(2,1)S(1)}, u32[]{:S(2)}, u32[]{:S(2)}) async-start(bf16[32,64,128]{2,1,0:T(8,128)(2,1)} %source_rows.1), calls=%async_computation.1 | async-start | bytes 1048576 | tf_op jit(solution)/shard_map/all_to_all | solution.py:332
  31.8 2.2 %copy-start.1 = (bf16[16,128,1024]{2,1,0:T(8,128)(2,1)S(1)}, bf16[16,128,1024]{2,1,0:T(8,128)(2,1)}, u32[]{:S(2)}) copy-start(bf16[16,128,1024]{2,1,0:T(8,128)(2,1)} %raw_ref.5) | copy-start | bytes 12582916
  39.0 1.3 %copy-start.3 = (bf16[64,2,4,16,128]{4,3,2,1,0:T(8,128)(2,1)}, bf16[64,2,4,16,128]{4,3,2,1,0:T(8,128)(2,1)S(1)}, u32[]{:S(2)}) copy-start(bf16[64,2,4,16,128]{4,3,2,1,0:T(8,128)(2,1)S(1)} %whiten1.1) | copy-start | bytes 6291460
  40.3 6.3 %copy-start.10 = (bf16[256,1024]{1,0:T(8,128)(2,1)S(1)}, bf16[256,1024]{1,0:T(8,128)(2,1)}, u32[]{:S(2)}) copy-start(bf16[256,1024]{1,0:T(8,128)(2,1)} %constant.5.clone.lag_ref) | copy-start | bytes 1572868
  45.3 1.3 %copy-start.5 = (bf16[64,2,4,16,128]{4,3,2,1,0:T(8,128)(2,1)}, bf16[64,2,4,16,128]{4,3,2,1,0:T(8,128)(2,1)S(1)}, u32[]{:S(2)}) copy-start(bf16[64,2,4,16,128]{4,3,2,1,0:T(8,128)(2,1)S(1)} %whiten0.1) | copy-start | bytes 6291460
  46.7 1.6 %copy-start.4 = (bf16[64,2,4,16,128]{4,3,2,1,0:T(8,128)(2,1)S(1)}, bf16[64,2,4,16,128]{4,3,2,1,0:T(8,128)(2,1)}, u32[]{:S(2)}) copy-start(bf16[64,2,4,16,128]{4,3,2,1,0:T(8,128)(2,1)} %copy-done.3) | copy-start | bytes 6291460
  48.2 1.6 %copy-start.6 = (bf16[64,2,4,16,128]{4,3,2,1,0:T(8,128)(2,1)S(1)}, bf16[64,2,4,16,128]{4,3,2,1,0:T(8,128)(2,1)}, u32[]{:S(2)}) copy-start(bf16[64,2,4,16,128]{4,3,2,1,0:T(8,128)(2,1)} %copy-done.5) | copy-start | bytes 6291460
  56.0 0.7 copy-start.7
  56.7 11.8 %collective-permute-start = (f32[16,32,128]{2,1,0:T(8,128)S(1)}, f32[16,32,128]{2,1,0:T(8,128)S(1)}, u32[]{:S(2)}, u32[]{:S(2)}) collective-permute-start(f32[16,32,128]{2,1,0:T(8,128)S(1)} %get-tuple-element.10), channel_id=1, source_target_pairs={{0,32},{32,0},{64,96},{96,64},{1,33},{33,1},{65,97},{97,65},{2,34}... | collective-permute-start | bytes 786440 | tf_op jit(solution)/shard_map/ppermute | solution.py:337
  58.8 6.6 %collective-permute-start.1 = (bf16[16,32,128]{2,1,0:T(8,128)(2,1)S(1)}, bf16[16,32,128]{2,1,0:T(8,128)(2,1)S(1)}, u32[]{:S(2)}, u32[]{:S(2)}) collective-permute-start(bf16[16,32,128]{2,1,0:T(8,128)(2,1)S(1)} %get-tuple-element.11), channel_id=1, source_target_pairs={{0,64},{32,96},{64,0},{96,32},{1,65},{33,97},{65,1},{97,33},{2,66}... | collective-permute-start | bytes 393224 | tf_op jit(solution)/shard_map/ppermute | solution.py:337
  61.3 7.2 %collective-permute-start.2 = (bf16[16,32,128]{2,1,0:T(8,128)(2,1)S(1)}, bf16[16,32,128]{2,1,0:T(8,128)(2,1)S(1)}, u32[]{:S(2)}, u32[]{:S(2)}) collective-permute-start(bf16[16,32,128]{2,1,0:T(8,128)(2,1)S(1)} %get-tuple-element.12), channel_id=1, source_target_pairs={{0,96},{32,64},{64,32},{96,0},{1,97},{33,65},{65,33},{97,1},{2,98}... | collective-permute-start | bytes 393224 | tf_op jit(solution)/shard_map/ppermute | solution.py:337
  65.5 3.0 %copy-start.12 = (bf16[16,32,128]{2,1,0:T(8,128)(2,1)}, bf16[16,32,128]{2,1,0:T(8,128)(2,1)S(1)}, u32[]{:S(2)}) copy-start(bf16[16,32,128]{2,1,0:T(8,128)(2,1)S(1)} %collective-permute-done.1.far0_ref) | copy-start | bytes 393220
  68.5 0.7 copy-start.13
  68.5 0.7 %copy-start.11 = (f32[16,32,128]{2,1,0:T(8,128)}, f32[16,32,128]{2,1,0:T(8,128)S(1)}, u32[]{:S(2)}) copy-start(f32[16,32,128]{2,1,0:T(8,128)S(1)} %collective-permute-done.core_ref) | copy-start | bytes 786436

commit v2 on v1

v2 whole, which is shorter than its diff:
```python
import functools

import jax
import jax.numpy as jnp
import ml_dtypes
import numpy as np
from jax import lax
from jax.experimental import pallas as pl
from jax.experimental.pallas import tpu as pltpu
from jax.sharding import PartitionSpec as P

SEGLEN = 1024
FREQS = 512
HALFLAG = 64
LAGS = 128
SMOOTH = 4
SOURCES = 16
PER_BLOCK = 4
WATER = 0.1
EPS = 1e-06

GROUPS = FREQS // 8
PICK_VMEM = 58 << 20
WHITEN_VMEM = 52 << 20
SOURCE_VMEM = 48 << 20
CORRELATE_VMEM = 52 << 20
SUM_VMEM = 14 << 20


def dft_rows():
    bins = np.arange(1, FREQS + 1)[:, None]
    times = np.arange(SEGLEN)[None, :]
    phase = ((bins * times) % SEGLEN).astype(np.float32) * np.float32(2.0 * np.pi / SEGLEN)
    table = np.concatenate([np.cos(phase), -np.sin(phase)], axis=0)
    return table.astype(ml_dtypes.bfloat16)


def lag_rows(scale):
    bins = np.arange(1, FREQS + 1)[None, :]
    lags = np.arange(LAGS)[:, None] - HALFLAG
    theta = ((bins * lags) % SEGLEN).astype(np.float32) * np.float32(2.0 * np.pi / SEGLEN)
    cos = np.cos(theta).reshape(LAGS, GROUPS, 1, 8)
    sin = np.sin(theta).reshape(LAGS, GROUPS, 1, 8)
    table = np.concatenate([cos, sin], axis=2).reshape(LAGS, 2 * FREQS) * np.float32(scale)
    high = table.astype(ml_dtypes.bfloat16)
    low = (table - high.astype(np.float32)).astype(ml_dtypes.bfloat16)
    return np.concatenate([high, low], axis=0)


def nt_dot(a, b):
    return lax.dot_general(a, b, (((1,), (1,)), ((), ())), preferred_element_type=jnp.float32)


def nn_dot(a, b):
    return lax.dot_general(a, b, (((1,), (0,)), ((), ())), preferred_element_type=jnp.float32)


def pick_body(index_ref, block_ref, raw_ref, out_ref, chan_ref, sel_ref, held_ref, sems):
    segs, count, _ = raw_ref.shape
    copies = []
    for i in range(segs // 2):
        part = pl.ds(2 * i, 2)
        copies.append(pltpu.make_async_copy(raw_ref.at[part], held_ref.at[part], sems.at[i]))
        copies[-1].start()
    first = lax.axis_index("ch") * count
    for s in range(SOURCES):
        rank = jnp.int32(0)
        for t in range(s):
            rank += jnp.where(block_ref[t] == block_ref[s], 1, 0).astype(jnp.int32)
        chan_ref[block_ref[s] * PER_BLOCK + rank] = index_ref[s] - first
    lane = lax.broadcasted_iota(jnp.int32, (8, count), 1)
    sub = lax.broadcasted_iota(jnp.int32, (8, count), 0)
    for q in range(SOURCES):
        hit = jnp.where(lane == chan_ref[q], 1.0, 0.0)
        for g in range(8):
            sel_ref[q * 8 : q * 8 + 8, g * count : (g + 1) * count] = jnp.where(sub == g, hit, 0.0)
    select = sel_ref[...].astype(jnp.bfloat16)
    for h in range(segs // 8):
        for i in range(4 * h, 4 * h + 4):
            copies[i].wait()
        rows = held_ref[8 * h : 8 * h + 8].reshape(8 * count, SEGLEN)
        out_ref[:, h] = nn_dot(select, rows).astype(jnp.bfloat16).reshape(SOURCES, 8, SEGLEN)


def pick(raw, source_index, source_block):
    segs, count, length = raw.shape
    return pl.pallas_call(
        pick_body,
        grid_spec=pltpu.PrefetchScalarGridSpec(
            num_scalar_prefetch=2,
            grid=(1,),
            in_specs=[pl.BlockSpec(memory_space=pl.ANY)],
            out_specs=pl.BlockSpec((SOURCES, segs // 8, 8, length), lambda i, *_: (0, 0, 0, 0)),
            scratch_shapes=[
                pltpu.SMEM((SOURCES,), jnp.int32),
                pltpu.VMEM((SOURCES * 8, 8 * count), jnp.float32),
                pltpu.VMEM(raw.shape, raw.dtype),
                pltpu.SemaphoreType.DMA((segs // 2,)),
            ],
        ),
        out_shape=jax.ShapeDtypeStruct((SOURCES, segs // 8, 8, length), jnp.bfloat16),
        compiler_params=pltpu.CompilerParams(vmem_limit_bytes=PICK_VMEM),
        cost_estimate=pl.CostEstimate(flops=2 * 10**8, bytes_accessed=5 * 10**6, transcendentals=0),
        name="pick",
    )(source_index, source_block, raw)


def source_body(parts_ref, table_ref, after_ref, out_ref):
    total = jnp.sum(parts_ref[...].astype(jnp.float32), axis=0)
    spectrum = nt_dot(total.astype(jnp.bfloat16), table_ref[...])
    real = spectrum[:, :FREQS]
    imag = spectrum[:, FREQS:]
    amplitude = jnp.sqrt(real * real + imag * imag)
    place = lax.broadcasted_iota(jnp.int32, amplitude.shape, 1)
    smoothed = amplitude
    for shift in range(1, SMOOTH + 1):
        later = pltpu.roll(amplitude, FREQS - shift, 1)
        smoothed += jnp.where(place < FREQS - shift, later, 0.0)
        earlier = pltpu.roll(amplitude, shift, 1)
        smoothed += jnp.where(place >= shift, earlier, 0.0)
    level = jnp.sum(amplitude, axis=1, keepdims=True) * (1.0 / FREQS)
    divisor = smoothed / (2 * SMOOTH + 1) + WATER * level + EPS
    real = (real / divisor).astype(jnp.bfloat16).astype(jnp.float32)
    imag = (imag / divisor).astype(jnp.bfloat16).astype(jnp.float32)
    sub = lax.broadcasted_iota(jnp.int32, (8, 128), 0)
    lane = lax.broadcasted_iota(jnp.int32, (8, 128), 1)
    block = (lane // 8) % 8

    def turn(x):
        for s in (4, 2, 1):
            down = pltpu.roll(pltpu.roll(x, s, 0), 128 - 8 * s, 1)
            up = pltpu.roll(pltpu.roll(x, 8 - s, 0), 8 * s, 1)
            low_row = (sub & s) == 0
            low_block = (block & s) == 0
            x = jnp.where(low_row == low_block, x, jnp.where(low_row, up, down))
        return x

    rows = []
    for j in range(FREQS // 128):
        re = turn(real[:, j * 128 : (j + 1) * 128])
        im = turn(imag[:, j * 128 : (j + 1) * 128])
        rows.append(jnp.where(lane < 64, re, pltpu.roll(im, 64, 1)))
        rows.append(jnp.where(lane < 64, pltpu.roll(re, 64, 1), im))
    packed = jnp.concatenate(rows, axis=0).astype(jnp.bfloat16)
    out_ref[...] = jnp.broadcast_to(packed[None], out_ref.shape)


def source_rows(parts, table, after):
    return pl.pallas_call(
        source_body,
        out_shape=jax.ShapeDtypeStruct((parts.shape[0], GROUPS, 128), jnp.bfloat16),
        in_specs=[pl.BlockSpec(memory_space=pltpu.VMEM)] * 2 + [pl.BlockSpec(memory_space=pl.ANY)],
        out_specs=pl.BlockSpec(memory_space=pltpu.VMEM),
        compiler_params=pltpu.CompilerParams(vmem_limit_bytes=SOURCE_VMEM),
        cost_estimate=pl.CostEstimate(flops=2 * 8 * 1024 * 1024, bytes_accessed=3 * 10**6, transcendentals=0),
        name="source_rows",
    )(parts, table, after)


def whiten_body(raw_ref, table_ref, out_ref, done_ref, spec_ref, amp_ref):
    count = raw_ref.shape[1]
    width = 2 * count
    step = 32
    size = step + 16
    zero = jnp.zeros((8, width), jnp.float32)
    done_ref[...] = zero[:, :128]
    amp_ref[0:8, :] = zero
    amp_ref[FREQS + 8 : FREQS + 16, :] = zero
    spec_ref[...] = nt_dot(table_ref[...], raw_ref[...].reshape(width, SEGLEN))
    level = zero
    for f in range(0, FREQS, step):
        real = spec_ref[f : f + step, :]
        imag = spec_ref[FREQS + f : FREQS + f + step, :]
        amplitude = jnp.sqrt(real * real + imag * imag)
        amp_ref[8 + f : 8 + f + step, :] = amplitude
        for i in range(0, step, 8):
            level += amplitude[i : i + 8]
    level = jnp.sum(level, axis=0, keepdims=True) * (WATER / FREQS) + EPS
    for f in range(0, FREQS, step):
        a = amp_ref[f : f + size, :]
        s2 = a + pltpu.roll(a, size - 1, 0)
        s4 = s2 + pltpu.roll(s2, size - 2, 0)
        s9 = s4 + pltpu.roll(s4, 4, 0) + pltpu.roll(a, size - 4, 0)
        inverse = 1.0 / (s9[8 : 8 + step] * (1.0 / (2 * SMOOTH + 1)) + level)
        real = spec_ref[f : f + step, :] * inverse
        imag = spec_ref[FREQS + f : FREQS + f + step, :] * inverse
        for part, value in ((0, real), (1, imag)):
            for i in range(0, step, 8):
                both = jnp.concatenate([value[i : i + 8, :count], value[i : i + 8, count:]], axis=0)
                out_ref[(f + i) // 8, part, 0] = both.astype(jnp.bfloat16)


def whiten(raw, table, half):
    segs, count, length = raw.shape
    pairs = segs // 4
    out, done = pl.pallas_call(
        whiten_body,
        grid=(pairs,),
        in_specs=[
            pl.BlockSpec((2, count, length), lambda i: (i + half * pairs, 0, 0)),
            pl.BlockSpec((2 * FREQS, length), lambda i: (0, 0)),
        ],
        out_specs=[
            pl.BlockSpec((GROUPS, 2, 1, 16, count), lambda i: (0, 0, i, 0, 0)),
            pl.BlockSpec((8, 128), lambda i: (0, 0)),
        ],
        out_shape=[
            jax.ShapeDtypeStruct((GROUPS, 2, pairs, 16, count), jnp.bfloat16),
            jax.ShapeDtypeStruct((8, 128), jnp.float32),
        ],
        scratch_shapes=[
            pltpu.VMEM((2 * FREQS, 2 * count), jnp.float32),
            pltpu.VMEM((FREQS + 16, 2 * count), jnp.float32),
        ],
        compiler_params=pltpu.CompilerParams(vmem_limit_bytes=WHITEN_VMEM),
        cost_estimate=pl.CostEstimate(
            flops=2 * 1024 * 1024 * 1024, bytes_accessed=6 * 10**6, transcendentals=10**6
        ),
        name=f"whiten{half}",
    )(raw, table)
    return out.reshape(GROUPS, 32 * pairs, count), done


def correlate_body(
    src_ref, w0_ref, w1_ref, lag_ref, mine_ref, core_ref, far0_ref, far1_ref,
    s_ref, w_ref, table_ref, high_ref, low_ref, sum_ref, sems, table_sem,
):
    count = w0_ref.shape[2]
    deep = w0_ref.shape[1]
    parts = sems.shape[0]
    blocks = GROUPS // parts

    def load(i, half):
        at = pl.ds(i * blocks, blocks)
        source = (w0_ref, w1_ref)[half]
        return pltpu.make_async_copy(
            source.at[at], w_ref.at[at, pl.ds(half * deep, deep)], sems.at[i, half]
        )

    for i in range(parts):
        load(i, 0).start()
        load(i, 1).start()
    table_copy = pltpu.make_async_copy(lag_ref, table_ref, table_sem)
    table_copy.start()

    lanes = lax.broadcasted_iota(jnp.int32, (GROUPS, 128), 1)
    for i in range(2 * SOURCES):
        value = src_ref[i].astype(jnp.float32)
        s_ref[0, i] = value
        turned = pltpu.roll(value, 64, 1)
        s_ref[1, i] = jnp.where(lanes < 64, -turned, turned)

    sub = lax.broadcasted_iota(jnp.int32, (8, 128), 0)
    lane = lax.broadcasted_iota(jnp.int32, (8, 128), 1)
    diagonal = (lane % 8) == sub

    def chunk(i, carry):
        load(i, 0).wait()
        load(i, 1).wait()
        for j in range(blocks):
            b = i * blocks + j
            tiles = []
            for q in range(SOURCES):
                halves = []
                for h in range(2):
                    pieces = []
                    for r in range(2):
                        row = jnp.broadcast_to(s_ref[r, 2 * q + h, pl.ds(b, 1), :], (8, 128))
                        pieces.append(jnp.where(diagonal, row, 0.0))
                    halves.append(jnp.concatenate(pieces, axis=0).astype(jnp.bfloat16))
                tiles.append(jnp.concatenate(halves, axis=1))
            cross = nn_dot(jnp.concatenate(tiles, axis=0), w_ref[b])
            high = cross.astype(jnp.bfloat16)
            low = (cross - high.astype(jnp.float32)).astype(jnp.bfloat16)
            at = pl.ds(pl.multiple_of(b * 16, 16), 16)
            for q in range(SOURCES):
                cols = slice((q % 2) * count, (q % 2 + 1) * count)
                high_ref[q // 2, at, cols] = high[q * 16 : q * 16 + 16]
                low_ref[q // 2, at, cols] = low[q * 16 : q * 16 + 16]
        return carry

    lax.fori_loop(0, parts, chunk, 0)
    table_copy.wait()
    me = lax.axis_index("seg")
    share = count // 4
    for p in range(SOURCES // 2):
        first = nn_dot(table_ref[...], high_ref[p])
        second = nn_dot(table_ref[:LAGS, :], low_ref[p])
        total = first[:LAGS] + (first[LAGS:] + second)
        for i in range(2):
            sum_ref[2 * p + i] = total[:, i * count : (i + 1) * count].T

    def part(r):
        return sum_ref[:, pl.ds(pl.multiple_of((me ^ r) * share, share), share), :]

    mine_ref[...] = part(0)
    core_ref[...] = part(1)
    far0_ref[...] = part(2).astype(jnp.bfloat16)
    far1_ref[...] = part(3).astype(jnp.bfloat16)


def correlate(src, w0, w1, lag):
    count = w0.shape[2]
    parts = 8
    share = count // 4
    shape = (SOURCES, share, LAGS)
    vmem = pl.BlockSpec(memory_space=pltpu.VMEM)
    anywhere = pl.BlockSpec(memory_space=pl.ANY)
    return pl.pallas_call(
        correlate_body,
        in_specs=[vmem, anywhere, anywhere, anywhere],
        out_specs=[vmem] * 4,
        out_shape=[
            jax.ShapeDtypeStruct(shape, jnp.float32),
            jax.ShapeDtypeStruct(shape, jnp.float32),
            jax.ShapeDtypeStruct(shape, jnp.bfloat16),
            jax.ShapeDtypeStruct(shape, jnp.bfloat16),
        ],
        scratch_shapes=[
            pltpu.VMEM((2, 2 * SOURCES, GROUPS, 128), jnp.float32),
            pltpu.VMEM((GROUPS, 2 * w0.shape[1], count), jnp.bfloat16),
            pltpu.VMEM(lag.shape, lag.dtype),
            pltpu.VMEM((SOURCES // 2, 2 * FREQS, 2 * count), jnp.bfloat16),
            pltpu.VMEM((SOURCES // 2, 2 * FREQS, 2 * count), jnp.bfloat16),
            pltpu.VMEM((SOURCES, count, LAGS), jnp.float32),
            pltpu.SemaphoreType.DMA((parts, 2)),
            pltpu.SemaphoreType.DMA,
        ],
        compiler_params=pltpu.CompilerParams(vmem_limit_bytes=CORRELATE_VMEM),
        cost_estimate=pl.CostEstimate(flops=3 * 10**9, bytes_accessed=6 * 10**6, transcendentals=0),
        name="correlate",
    )(src, w0, w1, lag)


def gather_sum_body(mine_ref, core_ref, far0_ref, far1_ref, out_ref):
    far = far0_ref[...].astype(jnp.float32) + far1_ref[...].astype(jnp.float32)
    total = (mine_ref[...] + core_ref[...]) + far
    for q in range(SOURCES):
        out_ref[:, q, :] = total[q]


def gather_sum(mine, core, far0, far1):
    shape = mine.shape
    return pl.pallas_call(
        gather_sum_body,
        in_specs=[pl.BlockSpec(memory_space=pltpu.VMEM)] * 4,
        out_specs=pl.BlockSpec(memory_space=pltpu.VMEM),
        out_shape=jax.ShapeDtypeStruct((shape[1], shape[0], shape[2]), jnp.float32),
        compiler_params=pltpu.CompilerParams(vmem_limit_bytes=SUM_VMEM),
        cost_estimate=pl.CostEstimate(flops=10**6, bytes_accessed=10**6, transcendentals=0),
        name="gather_sum",
    )(mine, core, far0, far1)


def local(raw, source_index, source_block):
    segs = raw.shape[0] * lax.axis_size("seg")
    ways = lax.axis_size("ch")
    table = jnp.asarray(dft_rows())
    lag = jnp.asarray(lag_rows(1.0 / (FREQS * segs)))
    picked = pick(raw, source_index, source_block)
    parts = lax.all_to_all(picked.reshape(ways, 8, SEGLEN), "ch", 0, 0)
    w0, done = whiten(raw, table, 0)
    spread = source_rows(parts, table, done)
    src = lax.all_to_all(spread, "ch", 0, 0)
    w1, _ = whiten(raw, table, 1)
    mine, core, far0, far1 = correlate(src, w0, w1, lag)

    def swap(x, r):
        return lax.ppermute(x, "seg", [(i, i ^ r) for i in range(4)])

    return gather_sum(mine, swap(core, 1), swap(far0, 2), swap(far1, 3))


def solution(mesh):
    return jax.shard_map(
        local,
        mesh=mesh,
        in_specs=(P("seg", "ch", None), P(), P()),
        out_specs=P(("ch", "seg"), None, None),
        check_vma=False,
    )
```

time: 71.6 us -> 62.6 us (0.87)
  blocking collectives: 20.7 us -> 0 us
  local copies, waits for them, and re-layouts: 12.9 us -> 0.01 us
  starting transfers between devices: 9.15 us -> 20 us
  Pallas kernels: 21.8 us -> 29 us
  waiting for transfers between devices: 6.5 us -> 13.1 us
    all_to_all x1 -> x0, blocking collectives: 20.7 us -> none  [local(): parts = lax.all_to_all(picked, 'ch', 0, 0)]
    unnamed x28 -> x4, local copies, waits for them, and re-layouts: 12.9 us -> 0.01 us
    all_to_all x0 -> x1, starting transfers between devices: none -> 9.83 us  [local(): parts = lax.all_to_all(picked.reshape(ways, 8, SEGLEN), 'ch', 0, 0)]
    pallas_call x2, Pallas kernels: 9.98 us -> 15 us  [whiten(): pl.pallas_call(whiten_body, grid=(pairs,), in_specs=[pl.BlockSpec((2, cou...]
    all_to_all x0 -> x1, waiting for transfers between devices: none -> 3.58 us  [local(): parts = lax.all_to_all(picked.reshape(ways, 8, SEGLEN), 'ch', 0, 0)]
    pallas_call x2, Pallas kernels: 7.93 us -> 11.2 us  [the longest x1 7.07 us: correlate(): pl.pallas_call(correlate_body, in_specs=[vmem, anywhere, anywhere, anywhe...]
    all_to_all x1, waiting for transfers between devices: 0.01 us -> 3.1 us  [local(): src = lax.all_to_all(spread, 'ch', 0, 0)]
    pallas_call x1, Pallas kernels: 1.97 us -> 0.88 us  [gather_sum(): pl.pallas_call(gather_sum_body, in_specs=[pl.BlockSpec(memory_space=pltpu...]
  transfers between devices with their start and end apart: 4 -> 5, of which waited for: 2 -> 4; matrix products, arithmetic and copies ran while one was open for 0% -> 0% of each run, Pallas kernels for 14% -> 24%
where the time goes in v2:
time: 62.6 us; the launch traced here: 62.2 us
  Pallas kernels  29 us (46%)
  starting transfers between devices  20 us (32%)
  waiting for transfers between devices  13.1 us (21%)
    pallas_call x2, Pallas kernels, whiten(): pl.pallas_call(whiten_body, grid=(pairs,), in_specs=[pl.BlockSpec((2, cou...  15 us
    all_to_all x1, starting transfers between devices, local(): parts = lax.all_to_all(picked.reshape(ways, 8, SEGLEN), 'ch', 0, 0)  9.83 us
    pallas_call x1, Pallas kernels, correlate(): pl.pallas_call(correlate_body, in_specs=[vmem, anywhere, anywhere, anywhe...  7.07 us
    ppermute x3, waiting for transfers between devices, swap(): return lax.ppermute(x, 'seg', [(i, i ^ r) for i in range(4)])  6.43 us
    ppermute x3, starting transfers between devices, swap(): return lax.ppermute(x, 'seg', [(i, i ^ r) for i in range(4)])  6.03 us
    all_to_all x1, starting transfers between devices, local(): src = lax.all_to_all(spread, 'ch', 0, 0)  4.15 us
    pallas_call x1, Pallas kernels, pick(): pl.pallas_call(pick_body, grid_spec=pltpu.PrefetchScalarGridSpec(num_scal...  4.13 us
    all_to_all x1, waiting for transfers between devices, local(): parts = lax.all_to_all(picked.reshape(ways, 8, SEGLEN), 'ch', 0, 0)  3.58 us
  transfers between devices with their start and end apart: 5, of which 4 were waited for; matrix products, arithmetic and copies ran while one was open for 0% of the time, Pallas kernels for 24%

profile of v2, /device:TPU:1, one launch (start us, length us, event | category | flops | bytes accessed | tf_op | source)
XLA Modules:
  0.0 62.2 jit_solution(14040617152119960303)
XLA Ops:
  0.0 4.1 %pick.1 = bf16[16,2,8,1024]{3,2,1,0:T(8,128)(2,1)} custom-call(s32[16]{0:T(128)} %index_ref.1, s32[16]{0:T(128)} %block_ref.1, bf16[16,128,1024]{2,1,0:T(8,128)(2,1)} %raw_ref.5), custom_call_target="tpu_custom_call" | custom-call | flops 200000000 | bytes 5000000 | tf_op jit(solution)/shard_map/pick/pallas_call | solution.py:87
  4.1 9.8 %all-to-all-start = ((bf16[32,8,1024]{2,1,0:T(8,128)(2,1)}), bf16[32,8,1024]{2,1,0:T(8,128)(2,1)S(1)}, u32[]{:S(2)}, u32[]{:S(2)}) async-start(bf16[32,8,1024]{2,1,0:T(8,128)(2,1)} %bitcast.3), calls=%async_computation | async-start | bytes 1048576 | tf_op jit(solution)/shard_map/all_to_all | solution.py:361
  14.0 0.0 copy-start
  14.0 7.5 %whiten0.1 = (bf16[64,2,4,16,128]{4,3,2,1,0:T(8,128)(2,1)}, f32[8,128]{1,0:T(8,128)S(1)}) custom-call(bf16[16,128,1024]{2,1,0:T(8,128)(2,1)} %raw_ref.5, bf16[1024,1024]{1,0:T(8,128)(2,1)} %constant.4.clone.table_ref), custom_call_target="tpu_custom_call" | custom-call | flops 2147483648 | bytes 6000000 | tf_op jit(solution)/shard_map/whiten0/pallas_call | solution.py:196
  21.5 3.6 %all-to-all-done.parts_ref = bf16[32,8,1024]{2,1,0:T(8,128)(2,1)S(1)} async-done(((bf16[32,8,1024]{2,1,0:T(8,128)(2,1)}), bf16[32,8,1024]{2,1,0:T(8,128)(2,1)S(1)}, u32[]{:S(2)}, u32[]{:S(2)}) %all-to-all-start) | async-done | bytes 524320 | tf_op jit(solution)/shard_map/all_to_all | solution.py:361
  25.1 0.0 copy-done
  25.1 1.9 %source_rows.1 = bf16[32,64,128]{2,1,0:T(8,128)(2,1)} custom-call(bf16[32,8,1024]{2,1,0:T(8,128)(2,1)S(1)} %all-to-all-done.parts_ref, bf16[1024,1024]{1,0:T(8,128)(2,1)S(1)} %copy-done, f32[8,128]{1,0:T(8,128)S(1)} %get-tuple-element.12.after_ref), custom_call_target="tpu_custom_call" | custom-call | flops 16777216 | bytes 3000000 | tf_op jit(solution)/shard_map/source_rows/pallas_call | solution.py:149
  27.0 4.2 %all-to-all-start.1 = ((bf16[32,64,128]{2,1,0:T(8,128)(2,1)}), bf16[32,64,128]{2,1,0:T(8,128)(2,1)S(1)}, u32[]{:S(2)}, u32[]{:S(2)}) async-start(bf16[32,64,128]{2,1,0:T(8,128)(2,1)} %source_rows.1), calls=%async_computation.1 | async-start | bytes 1048576 | tf_op jit(solution)/shard_map/all_to_all | solution.py:364
  31.2 0.0 copy-start.1
  31.2 7.4 %whiten1.1 = (bf16[64,2,4,16,128]{4,3,2,1,0:T(8,128)(2,1)}, f32[8,128]{1,0:T(8,128)}) custom-call(bf16[16,128,1024]{2,1,0:T(8,128)(2,1)} %raw_ref.5, bf16[1024,1024]{1,0:T(8,128)(2,1)} %constant.4.clone.table_ref), custom_call_target="tpu_custom_call" | custom-call | flops 2147483648 | bytes 6000000 | tf_op jit(solution)/shard_map/whiten1/pallas_call | solution.py:196
  38.7 3.1 %all-to-all-done.1.src_ref = bf16[32,64,128]{2,1,0:T(8,128)(2,1)S(1)} async-done(((bf16[32,64,128]{2,1,0:T(8,128)(2,1)}), bf16[32,64,128]{2,1,0:T(8,128)(2,1)S(1)}, u32[]{:S(2)}, u32[]{:S(2)}) %all-to-all-start.1) | async-done | bytes 524320 | tf_op jit(solution)/shard_map/all_to_all | solution.py:364
  41.8 0.0 copy-done.1
  41.8 7.1 %correlate.1 = (f32[16,32,128]{2,1,0:T(8,128)S(1)}, f32[16,32,128]{2,1,0:T(8,128)S(1)}, bf16[16,32,128]{2,1,0:T(8,128)(2,1)S(1)}, bf16[16,32,128]{2,1,0:T(8,128)(2,1)S(1)}) custom-call(bf16[32,64,128]{2,1,0:T(8,128)(2,1)S(1)} %all-to-all-done.1.src_ref, bf16[64,128,128]{2,1,0:T(8,128)(2,1)} %bitcast.4, bf16[64,128,128]{2,1,0:T(8,128)(2,1)} %bitcast.5, ...), custom_call_target="tpu_custom_call" | custom-call | flops 3000000000 | bytes 6000000 | tf_op jit(solution)/shard_map/correlate/pallas_call | solution.py:309
  48.8 2.8 %collective-permute-start = (f32[16,32,128]{2,1,0:T(8,128)S(1)}, f32[16,32,128]{2,1,0:T(8,128)S(1)}, u32[]{:S(2)}, u32[]{:S(2)}) collective-permute-start(f32[16,32,128]{2,1,0:T(8,128)S(1)} %get-tuple-element.16), channel_id=1, source_target_pairs={{0,32},{32,0},{64,96},{96,64},{1,33},{33,1},{65,97},{97,65},{2,34}... | collective-permute-start | bytes 786440 | tf_op jit(solution)/shard_map/ppermute | solution.py:369
  51.6 2.4 %collective-permute-start.1 = (bf16[16,32,128]{2,1,0:T(8,128)(2,1)S(1)}, bf16[16,32,128]{2,1,0:T(8,128)(2,1)S(1)}, u32[]{:S(2)}, u32[]{:S(2)}) collective-permute-start(bf16[16,32,128]{2,1,0:T(8,128)(2,1)S(1)} %get-tuple-element.17), channel_id=1, source_target_pairs={{0,64},{32,96},{64,0},{96,32},{1,65},{33,97},{65,1},{97,33},{2,66}... | collective-permute-start | bytes 393224 | tf_op jit(solution)/shard_map/ppermute | solution.py:369
  54.1 0.8 %collective-permute-start.2 = (bf16[16,32,128]{2,1,0:T(8,128)(2,1)S(1)}, bf16[16,32,128]{2,1,0:T(8,128)(2,1)S(1)}, u32[]{:S(2)}, u32[]{:S(2)}) collective-permute-start(bf16[16,32,128]{2,1,0:T(8,128)(2,1)S(1)} %get-tuple-element.18), channel_id=1, source_target_pairs={{0,96},{32,64},{64,32},{96,0},{1,97},{33,65},{65,33},{97,1},{2,98}... | collective-permute-start | bytes 393224 | tf_op jit(solution)/shard_map/ppermute | solution.py:369
  54.9 3.3 %collective-permute-done.1.far0_ref = bf16[16,32,128]{2,1,0:T(8,128)(2,1)S(1)} collective-permute-done((bf16[16,32,128]{2,1,0:T(8,128)(2,1)S(1)}, bf16[16,32,128]{2,1,0:T(8,128)(2,1)S(1)}, u32[]{:S(2)}, u32[]{:S(2)}) %collective-permute-start.1) | collective-permute-done | bytes 131104 | tf_op jit(solution)/shard_map/ppermute | solution.py:369
  58.2 3.1 %collective-permute-done.2.far1_ref = bf16[16,32,128]{2,1,0:T(8,128)(2,1)S(1)} collective-permute-done((bf16[16,32,128]{2,1,0:T(8,128)(2,1)S(1)}, bf16[16,32,128]{2,1,0:T(8,128)(2,1)S(1)}, u32[]{:S(2)}, u32[]{:S(2)}) %collective-permute-start.2) | collective-permute-done | bytes 131104 | tf_op jit(solution)/shard_map/ppermute | solution.py:369
  61.3 0.0 collective-permute-done.core_ref
  61.3 0.9 %gather_sum.1 = f32[32,16,128]{2,1,0:T(8,128)} custom-call(f32[16,32,128]{2,1,0:T(8,128)S(1)} %get-tuple-element.15.mine_ref, f32[16,32,128]{2,1,0:T(8,128)S(1)} %collective-permute-done.core_ref, bf16[16,32,128]{2,1,0:T(8,128)(2,1)S(1)} %collective-permute-done.1.far0_ref, bf16[16,32,128]{2,1,0:T(8,128)(2,1)S(1)} %collective-permute-done.2.far1_ref), custom_call_target="tpu_custom_call" | custom-call | flops 1000000 | bytes 1000000 | tf_op jit(solution)/shard_map/gather_sum/pallas_call | solution.py:344
Async XLA Ops:
  4.1 21.0 %all-to-all-start = ((bf16[32,8,1024]{2,1,0:T(8,128)(2,1)}), bf16[32,8,1024]{2,1,0:T(8,128)(2,1)S(1)}, u32[]{:S(2)}, u32[]{:S(2)}) async-start(bf16[32,8,1024]{2,1,0:T(8,128)(2,1)} %bitcast.3), calls=%async_computation | async-start | bytes 1048576 | tf_op jit(solution)/shard_map/all_to_all | solution.py:361
  14.0 11.1 %copy-start = (bf16[1024,1024]{1,0:T(8,128)(2,1)S(1)}, bf16[1024,1024]{1,0:T(8,128)(2,1)}, u32[]{:S(2)}) copy-start(bf16[1024,1024]{1,0:T(8,128)(2,1)} %constant.4.clone.table_ref) | copy-start | bytes 6291460
  27.0 14.7 %all-to-all-start.1 = ((bf16[32,64,128]{2,1,0:T(8,128)(2,1)}), bf16[32,64,128]{2,1,0:T(8,128)(2,1)S(1)}, u32[]{:S(2)}, u32[]{:S(2)}) async-start(bf16[32,64,128]{2,1,0:T(8,128)(2,1)} %source_rows.1), calls=%async_computation.1 | async-start | bytes 1048576 | tf_op jit(solution)/shard_map/all_to_all | solution.py:364
  31.2 10.6 %copy-start.1 = (bf16[256,1024]{1,0:T(8,128)(2,1)S(1)}, bf16[256,1024]{1,0:T(8,128)(2,1)}, u32[]{:S(2)}) copy-start(bf16[256,1024]{1,0:T(8,128)(2,1)} %constant.5.clone.lag_ref) | copy-start | bytes 1572868
  48.8 12.5 %collective-permute-start = (f32[16,32,128]{2,1,0:T(8,128)S(1)}, f32[16,32,128]{2,1,0:T(8,128)S(1)}, u32[]{:S(2)}, u32[]{:S(2)}) collective-permute-start(f32[16,32,128]{2,1,0:T(8,128)S(1)} %get-tuple-element.16), channel_id=1, source_target_pairs={{0,32},{32,0},{64,96},{96,64},{1,33},{33,1},{65,97},{97,65},{2,34}... | collective-permute-start | bytes 786440 | tf_op jit(solution)/shard_map/ppermute | solution.py:369
  51.6 6.6 %collective-permute-start.1 = (bf16[16,32,128]{2,1,0:T(8,128)(2,1)S(1)}, bf16[16,32,128]{2,1,0:T(8,128)(2,1)S(1)}, u32[]{:S(2)}, u32[]{:S(2)}) collective-permute-start(bf16[16,32,128]{2,1,0:T(8,128)(2,1)S(1)} %get-tuple-element.17), channel_id=1, source_target_pairs={{0,64},{32,96},{64,0},{96,32},{1,65},{33,97},{65,1},{97,33},{2,66}... | collective-permute-start | bytes 393224 | tf_op jit(solution)/shard_map/ppermute | solution.py:369
  54.1 7.2 %collective-permute-start.2 = (bf16[16,32,128]{2,1,0:T(8,128)(2,1)S(1)}, bf16[16,32,128]{2,1,0:T(8,128)(2,1)S(1)}, u32[]{:S(2)}, u32[]{:S(2)}) collective-permute-start(bf16[16,32,128]{2,1,0:T(8,128)(2,1)S(1)} %get-tuple-element.18), channel_id=1, source_target_pairs={{0,96},{32,64},{64,32},{96,0},{1,97},{33,65},{65,33},{97,1},{2,98}... | collective-permute-start | bytes 393224 | tf_op jit(solution)/shard_map/ppermute | solution.py:369

commit v3 on v2

--- a/solution.py
+++ b/solution.py
@@ -55,12 +55,14 @@
     return lax.dot_general(a, b, (((1,), (0,)), ((), ())), preferred_element_type=jnp.float32)
 
 
-def pick_body(index_ref, block_ref, raw_ref, out_ref, chan_ref, sel_ref, held_ref, sems):
+def pick_body(index_ref, block_ref, raw_ref, out_ref, chan_ref, sel_ref, held_ref, got_ref, sems, out_sems):
     segs, count, _ = raw_ref.shape
+    parts = sems.shape[0]
+    size = segs // parts
     copies = []
-    for i in range(segs // 2):
-        part = pl.ds(2 * i, 2)
-        copies.append(pltpu.make_async_copy(raw_ref.at[part], held_ref.at[part], sems.at[i]))
+    for i in range(parts):
+        at = pl.ds(i * size, size)
+        copies.append(pltpu.make_async_copy(raw_ref.at[at], held_ref.at[at], sems.at[i]))
         copies[-1].start()
     first = lax.axis_index("ch") * count
     for s in range(SOURCES):
@@ -75,27 +77,39 @@
         for g in range(8):
             sel_ref[q * 8 : q * 8 + 8, g * count : (g + 1) * count] = jnp.where(sub == g, hit, 0.0)
     select = sel_ref[...].astype(jnp.bfloat16)
+    outs = []
     for h in range(segs // 8):
-        for i in range(4 * h, 4 * h + 4):
+        total = None
+        for i in range(8 * h // size, (8 * h + 8) // size):
             copies[i].wait()
-        rows = held_ref[8 * h : 8 * h + 8].reshape(8 * count, SEGLEN)
-        out_ref[:, h] = nn_dot(select, rows).astype(jnp.bfloat16).reshape(SOURCES, 8, SEGLEN)
+            rows = held_ref[i * size : (i + 1) * size].reshape(size * count, SEGLEN)
+            g = (i * size) % 8
+            term = nn_dot(select[:, g * count : (g + size) * count], rows)
+            total = term if total is None else total + term
+        got_ref[h] = total.astype(jnp.bfloat16).reshape(SOURCES, 8, SEGLEN)
+        outs.append(pltpu.make_async_copy(got_ref.at[h], out_ref.at[:, h], out_sems.at[h]))
+        outs[-1].start()
+    for copy in outs:
+        copy.wait()
 
 
 def pick(raw, source_index, source_block):
     segs, count, length = raw.shape
+    parts = 8
     return pl.pallas_call(
         pick_body,
         grid_spec=pltpu.PrefetchScalarGridSpec(
             num_scalar_prefetch=2,
             grid=(1,),
             in_specs=[pl.BlockSpec(memory_space=pl.ANY)],
-            out_specs=pl.BlockSpec((SOURCES, segs // 8, 8, length), lambda i, *_: (0, 0, 0, 0)),
+            out_specs=pl.BlockSpec(memory_space=pl.ANY),
             scratch_shapes=[
                 pltpu.SMEM((SOURCES,), jnp.int32),
                 pltpu.VMEM((SOURCES * 8, 8 * count), jnp.float32),
                 pltpu.VMEM(raw.shape, raw.dtype),
-                pltpu.SemaphoreType.DMA((segs // 2,)),
+                pltpu.VMEM((segs // 8, SOURCES, 8, length), raw.dtype),
+                pltpu.SemaphoreType.DMA((parts,)),
+                pltpu.SemaphoreType.DMA((segs // 8,)),
             ],
         ),
         out_shape=jax.ShapeDtypeStruct((SOURCES, segs // 8, 8, length), jnp.bfloat16),
@@ -221,10 +235,9 @@
     return out.reshape(GROUPS, 32 * pairs, count), done
 
 
-def correlate_body(
-    src_ref, w0_ref, w1_ref, lag_ref, mine_ref, core_ref, far0_ref, far1_ref,
-    s_ref, w_ref, table_ref, high_ref, low_ref, sum_ref, sems, table_sem,
-):
+def correlate_body(src_ref, w0_ref, w1_ref, lag_ref, *refs):
+    out_refs = refs[:4]
+    s_ref, w_ref, table_ref, high_ref, low_ref, sum_ref, sems, table_sem = refs[4:]
     count = w0_ref.shape[2]
     deep = w0_ref.shape[1]
     parts = sems.shape[0]
@@ -293,10 +306,8 @@
     def part(r):
         return sum_ref[:, pl.ds(pl.multiple_of((me ^ r) * share, share), share), :]
 
-    mine_ref[...] = part(0)
-    core_ref[...] = part(1)
-    far0_ref[...] = part(2).astype(jnp.bfloat16)
-    far1_ref[...] = part(3).astype(jnp.bfloat16)
+    for r, out_ref in enumerate(out_refs):
+        out_ref[...] = part(r)
 
 
 def correlate(src, w0, w1, lag):
@@ -310,12 +321,7 @@
         correlate_body,
         in_specs=[vmem, anywhere, anywhere, anywhere],
         out_specs=[vmem] * 4,
-        out_shape=[
-            jax.ShapeDtypeStruct(shape, jnp.float32),
-            jax.ShapeDtypeStruct(shape, jnp.float32),
-            jax.ShapeDtypeStruct(shape, jnp.bfloat16),
-            jax.ShapeDtypeStruct(shape, jnp.bfloat16),
-        ],
+        out_shape=[jax.ShapeDtypeStruct(shape, jnp.float32)] * 4,
         scratch_shapes=[
             pltpu.VMEM((2, 2 * SOURCES, GROUPS, 128), jnp.float32),
             pltpu.VMEM((GROUPS, 2 * w0.shape[1], count), jnp.bfloat16),
@@ -332,24 +338,39 @@
     )(src, w0, w1, lag)
 
 
-def gather_sum_body(mine_ref, core_ref, far0_ref, far1_ref, out_ref):
-    far = far0_ref[...].astype(jnp.float32) + far1_ref[...].astype(jnp.float32)
-    total = (mine_ref[...] + core_ref[...]) + far
+def chip_sum_body(mine_ref, core_ref, out_ref):
+    out_ref[...] = (mine_ref[...] + core_ref[...]).astype(jnp.bfloat16)
+
+
+def chip_sum(mine, core):
+    return pl.pallas_call(
+        chip_sum_body,
+        in_specs=[pl.BlockSpec(memory_space=pltpu.VMEM)] * 2,
+        out_specs=pl.BlockSpec(memory_space=pltpu.VMEM),
+        out_shape=jax.ShapeDtypeStruct(mine.shape, jnp.bfloat16),
+        compiler_params=pltpu.CompilerParams(vmem_limit_bytes=SUM_VMEM),
+        cost_estimate=pl.CostEstimate(flops=10**5, bytes_accessed=10**6, transcendentals=0),
+        name="chip_sum",
+    )(mine, core)
+
+
+def gather_sum_body(mine_ref, core_ref, far_ref, out_ref):
+    total = (mine_ref[...] + core_ref[...]) + far_ref[...].astype(jnp.float32)
     for q in range(SOURCES):
         out_ref[:, q, :] = total[q]
 
 
-def gather_sum(mine, core, far0, far1):
+def gather_sum(mine, core, far):
     shape = mine.shape
     return pl.pallas_call(
         gather_sum_body,
-        in_specs=[pl.BlockSpec(memory_space=pltpu.VMEM)] * 4,
+        in_specs=[pl.BlockSpec(memory_space=pltpu.VMEM)] * 3,
         out_specs=pl.BlockSpec(memory_space=pltpu.VMEM),
         out_shape=jax.ShapeDtypeStruct((shape[1], shape[0], shape[2]), jnp.float32),
         compiler_params=pltpu.CompilerParams(vmem_limit_bytes=SUM_VMEM),
         cost_estimate=pl.CostEstimate(flops=10**6, bytes_accessed=10**6, transcendentals=0),
         name="gather_sum",
-    )(mine, core, far0, far1)
+    )(mine, core, far)
 
 
 def local(raw, source_index, source_block):
@@ -363,12 +384,13 @@
     spread = source_rows(parts, table, done)
     src = lax.all_to_all(spread, "ch", 0, 0)
     w1, _ = whiten(raw, table, 1)
-    mine, core, far0, far1 = correlate(src, w0, w1, lag)
+    parts = correlate(src, w0, w1, lag)
 
     def swap(x, r):
         return lax.ppermute(x, "seg", [(i, i ^ r) for i in range(4)])
 
-    return gather_sum(mine, swap(core, 1), swap(far0, 2), swap(far1, 3))
+    far = swap(chip_sum(parts[2], swap(parts[3], 1)), 2)
+    return gather_sum(parts[0], swap(parts[1], 1), far)
 
 
 def solution(mesh):

time: 62.6 us -> 60.3 us (0.963)
  waiting for transfers between devices: 13.1 us -> 11.5 us
    ppermute x3, waiting for transfers between devices: 6.43 us -> 4.82 us  [swap(): return lax.ppermute(x, 'seg', [(i, i ^ r) for i in range(4)])]
  transfers between devices with their start and end apart: 5 -> 5, of which waited for: 4 -> 4; matrix products, arithmetic and copies ran while one was open for 0% -> 0% of each run, Pallas kernels for 24% -> 25%
where the time goes in v3:
time: 60.3 us; the launch traced here: 59.8 us
  Pallas kernels  28.8 us (48%)
  starting transfers between devices  19.4 us (32%)
  waiting for transfers between devices  11.5 us (19%)
    pallas_call x2, Pallas kernels, whiten(): pl.pallas_call(whiten_body, grid=(pairs,), in_specs=[pl.BlockSpec((2, cou...  14.9 us
    all_to_all x1, starting transfers between devices, local(): parts = lax.all_to_all(picked.reshape(ways, 8, SEGLEN), 'ch', 0, 0)  9.82 us
    pallas_call x1, Pallas kernels, correlate(): pl.pallas_call(correlate_body, in_specs=[vmem, anywhere, anywhere, anywhe...  7.16 us
    ppermute x3, starting transfers between devices, swap(): return lax.ppermute(x, 'seg', [(i, i ^ r) for i in range(4)])  5.41 us
    ppermute x3, waiting for transfers between devices, swap(): return lax.ppermute(x, 'seg', [(i, i ^ r) for i in range(4)])  4.82 us
    all_to_all x1, starting transfers between devices, local(): src = lax.all_to_all(spread, 'ch', 0, 0)  4.16 us
    pallas_call x1, Pallas kernels, pick(): pl.pallas_call(pick_body, grid_spec=pltpu.PrefetchScalarGridSpec(num_scal...  3.89 us
    all_to_all x1, waiting for transfers between devices, local(): parts = lax.all_to_all(picked.reshape(ways, 8, SEGLEN), 'ch', 0, 0)  3.57 us
  transfers between devices with their start and end apart: 5, of which 4 were waited for; matrix products, arithmetic and copies ran while one was open for 0% of the time, Pallas kernels for 25%

profile of v3, /device:TPU:1, one launch (start us, length us, event | category | flops | bytes accessed | tf_op | source)
XLA Modules:
  0.0 59.8 jit_solution(4109077730531182559)
XLA Ops:
  0.0 3.9 %pick.1 = bf16[16,2,8,1024]{3,2,1,0:T(8,128)(2,1)} custom-call(s32[16]{0:T(128)} %index_ref.1, s32[16]{0:T(128)} %block_ref.1, bf16[16,128,1024]{2,1,0:T(8,128)(2,1)} %raw_ref.5), custom_call_target="tpu_custom_call" | custom-call | flops 200000000 | bytes 5000000 | tf_op jit(solution)/shard_map/pick/pallas_call | solution.py:99
  3.9 9.8 %all-to-all-start = ((bf16[32,8,1024]{2,1,0:T(8,128)(2,1)}), bf16[32,8,1024]{2,1,0:T(8,128)(2,1)S(1)}, u32[]{:S(2)}, u32[]{:S(2)}) async-start(bf16[32,8,1024]{2,1,0:T(8,128)(2,1)} %bitcast.3), calls=%async_computation | async-start | bytes 1048576 | tf_op jit(solution)/shard_map/all_to_all | solution.py:382
  13.7 0.0 copy-start
  13.7 7.5 %whiten0.1 = (bf16[64,2,4,16,128]{4,3,2,1,0:T(8,128)(2,1)}, f32[8,128]{1,0:T(8,128)S(1)}) custom-call(bf16[16,128,1024]{2,1,0:T(8,128)(2,1)} %raw_ref.5, bf16[1024,1024]{1,0:T(8,128)(2,1)} %constant.4.clone.table_ref), custom_call_target="tpu_custom_call" | custom-call | flops 2147483648 | bytes 6000000 | tf_op jit(solution)/shard_map/whiten0/pallas_call | solution.py:210
  21.3 3.6 %all-to-all-done.parts_ref = bf16[32,8,1024]{2,1,0:T(8,128)(2,1)S(1)} async-done(((bf16[32,8,1024]{2,1,0:T(8,128)(2,1)}), bf16[32,8,1024]{2,1,0:T(8,128)(2,1)S(1)}, u32[]{:S(2)}, u32[]{:S(2)}) %all-to-all-start) | async-done | bytes 524320 | tf_op jit(solution)/shard_map/all_to_all | solution.py:382
  24.8 0.0 copy-done
  24.8 1.9 %source_rows.1 = bf16[32,64,128]{2,1,0:T(8,128)(2,1)} custom-call(bf16[32,8,1024]{2,1,0:T(8,128)(2,1)S(1)} %all-to-all-done.parts_ref, bf16[1024,1024]{1,0:T(8,128)(2,1)S(1)} %copy-done, f32[8,128]{1,0:T(8,128)S(1)} %get-tuple-element.12.after_ref), custom_call_target="tpu_custom_call" | custom-call | flops 16777216 | bytes 3000000 | tf_op jit(solution)/shard_map/source_rows/pallas_call | solution.py:163
  26.8 4.2 %all-to-all-start.1 = ((bf16[32,64,128]{2,1,0:T(8,128)(2,1)}), bf16[32,64,128]{2,1,0:T(8,128)(2,1)S(1)}, u32[]{:S(2)}, u32[]{:S(2)}) async-start(bf16[32,64,128]{2,1,0:T(8,128)(2,1)} %source_rows.1), calls=%async_computation.1 | async-start | bytes 1048576 | tf_op jit(solution)/shard_map/all_to_all | solution.py:385
  31.0 7.4 %whiten1.1 = (bf16[64,2,4,16,128]{4,3,2,1,0:T(8,128)(2,1)}, f32[8,128]{1,0:T(8,128)}) custom-call(bf16[16,128,1024]{2,1,0:T(8,128)(2,1)} %raw_ref.5, bf16[1024,1024]{1,0:T(8,128)(2,1)} %constant.4.clone.table_ref), custom_call_target="tpu_custom_call" | custom-call | flops 2147483648 | bytes 6000000 | tf_op jit(solution)/shard_map/whiten1/pallas_call | solution.py:210
  38.4 3.2 %all-to-all-done.1.src_ref = bf16[32,64,128]{2,1,0:T(8,128)(2,1)S(1)} async-done(((bf16[32,64,128]{2,1,0:T(8,128)(2,1)}), bf16[32,64,128]{2,1,0:T(8,128)(2,1)S(1)}, u32[]{:S(2)}, u32[]{:S(2)}) %all-to-all-start.1) | async-done | bytes 524320 | tf_op jit(solution)/shard_map/all_to_all | solution.py:385
  41.5 7.2 %correlate.1 = (f32[16,32,128]{2,1,0:T(8,128)S(1)}, f32[16,32,128]{2,1,0:T(8,128)S(1)}, f32[16,32,128]{2,1,0:T(8,128)S(1)}, f32[16,32,128]{2,1,0:T(8,128)S(1)}) custom-call(bf16[32,64,128]{2,1,0:T(8,128)(2,1)S(1)} %all-to-all-done.1.src_ref, bf16[64,128,128]{2,1,0:T(8,128)(2,1)} %bitcast.4, bf16[64,128,128]{2,1,0:T(8,128)(2,1)} %bitcast.5, ...), custom_call_target="tpu_custom_call" | custom-call | flops 3000000000 | bytes 6000000 | tf_op jit(solution)/shard_map/correlate/pallas_call | solution.py:320
  48.7 2.8 %collective-permute-start.1 = (f32[16,32,128]{2,1,0:T(8,128)S(1)}, f32[16,32,128]{2,1,0:T(8,128)S(1)}, u32[]{:S(2)}, u32[]{:S(2)}) collective-permute-start(f32[16,32,128]{2,1,0:T(8,128)S(1)} %get-tuple-element.18), channel_id=1, source_target_pairs={{0,32},{32,0},{64,96},{96,64},{1,33},{33,1},{65,97},{97,65},{2,34}... | collective-permute-start | bytes 786440 | tf_op jit(solution)/shard_map/ppermute | solution.py:390
  51.5 0.1 collective-permute-start
  51.6 1.1 %collective-permute-done.1.core_ref = f32[16,32,128]{2,1,0:T(8,128)S(1)} collective-permute-done((f32[16,32,128]{2,1,0:T(8,128)S(1)}, f32[16,32,128]{2,1,0:T(8,128)S(1)}, u32[]{:S(2)}, u32[]{:S(2)}) %collective-permute-start.1) | collective-permute-done | bytes 262176 | tf_op jit(solution)/shard_map/ppermute | solution.py:390
  52.7 2.5 %collective-permute-start.2 = (bf16[16,32,128]{2,1,0:T(8,128)(2,1)S(1)}, bf16[16,32,128]{2,1,0:T(8,128)(2,1)S(1)}, u32[]{:S(2)}, u32[]{:S(2)}) collective-permute-start(bf16[16,32,128]{2,1,0:T(8,128)(2,1)S(1)} %chip_sum.1), channel_id=1, source_target_pairs={{0,64},{32,96},{64,0},{96,32},{1,65},{33,97},{65,1},{97,33},{2,66}... | collective-permute-start | bytes 393224 | tf_op jit(solution)/shard_map/ppermute | solution.py:390
  55.2 0.0 collective-permute-done.core_ref
  55.2 3.8 %collective-permute-done.2.far_ref = bf16[16,32,128]{2,1,0:T(8,128)(2,1)S(1)} collective-permute-done((bf16[16,32,128]{2,1,0:T(8,128)(2,1)S(1)}, bf16[16,32,128]{2,1,0:T(8,128)(2,1)S(1)}, u32[]{:S(2)}, u32[]{:S(2)}) %collective-permute-start.2) | collective-permute-done | bytes 131104 | tf_op jit(solution)/shard_map/ppermute | solution.py:390
  59.0 0.9 %gather_sum.1 = f32[32,16,128]{2,1,0:T(8,128)} custom-call(f32[16,32,128]{2,1,0:T(8,128)S(1)} %get-tuple-element.15.mine_ref, f32[16,32,128]{2,1,0:T(8,128)S(1)} %collective-permute-done.core_ref, bf16[16,32,128]{2,1,0:T(8,128)(2,1)S(1)} %collective-permute-done.2.far_ref), custom_call_target="tpu_custom_call" | custom-call | flops 1000000 | bytes 1000000 | tf_op jit(solution)/shard_map/gather_sum/pallas_call | solution.py:365
  (1 shorter events, 0.0 us)
Async XLA Ops:
  3.9 20.9 %all-to-all-start = ((bf16[32,8,1024]{2,1,0:T(8,128)(2,1)}), bf16[32,8,1024]{2,1,0:T(8,128)(2,1)S(1)}, u32[]{:S(2)}, u32[]{:S(2)}) async-start(bf16[32,8,1024]{2,1,0:T(8,128)(2,1)} %bitcast.3), calls=%async_computation | async-start | bytes 1048576 | tf_op jit(solution)/shard_map/all_to_all | solution.py:382
  13.7 11.1 %copy-start = (bf16[1024,1024]{1,0:T(8,128)(2,1)S(1)}, bf16[1024,1024]{1,0:T(8,128)(2,1)}, u32[]{:S(2)}) copy-start(bf16[1024,1024]{1,0:T(8,128)(2,1)} %constant.4.clone.table_ref) | copy-start | bytes 6291460
  26.8 14.7 %all-to-all-start.1 = ((bf16[32,64,128]{2,1,0:T(8,128)(2,1)}), bf16[32,64,128]{2,1,0:T(8,128)(2,1)S(1)}, u32[]{:S(2)}, u32[]{:S(2)}) async-start(bf16[32,64,128]{2,1,0:T(8,128)(2,1)} %source_rows.1), calls=%async_computation.1 | async-start | bytes 1048576 | tf_op jit(solution)/shard_map/all_to_all | solution.py:385
  48.7 3.9 %collective-permute-start.1 = (f32[16,32,128]{2,1,0:T(8,128)S(1)}, f32[16,32,128]{2,1,0:T(8,128)S(1)}, u32[]{:S(2)}, u32[]{:S(2)}) collective-permute-start(f32[16,32,128]{2,1,0:T(8,128)S(1)} %get-tuple-element.18), channel_id=1, source_target_pairs={{0,32},{32,0},{64,96},{96,64},{1,33},{33,1},{65,97},{97,65},{2,34}... | collective-permute-start | bytes 786440 | tf_op jit(solution)/shard_map/ppermute | solution.py:390
  51.5 3.7 %collective-permute-start = (f32[16,32,128]{2,1,0:T(8,128)S(1)}, f32[16,32,128]{2,1,0:T(8,128)S(1)}, u32[]{:S(2)}, u32[]{:S(2)}) collective-permute-start(f32[16,32,128]{2,1,0:T(8,128)S(1)} %get-tuple-element.16), channel_id=1, source_target_pairs={{0,32},{32,0},{64,96},{96,64},{1,33},{33,1},{65,97},{97,65},{2,34}... | collective-permute-start | bytes 786440 | tf_op jit(solution)/shard_map/ppermute | solution.py:390
  52.7 6.3 %collective-permute-start.2 = (bf16[16,32,128]{2,1,0:T(8,128)(2,1)S(1)}, bf16[16,32,128]{2,1,0:T(8,128)(2,1)S(1)}, u32[]{:S(2)}, u32[]{:S(2)}) collective-permute-start(bf16[16,32,128]{2,1,0:T(8,128)(2,1)S(1)} %chip_sum.1), channel_id=1, source_target_pairs={{0,64},{32,96},{64,0},{96,32},{1,65},{33,97},{65,1},{97,33},{2,66}... | collective-permute-start | bytes 393224 | tf_op jit(solution)/shard_map/ppermute | solution.py:390

commit v4 on v3

--- a/solution.py
+++ b/solution.py
@@ -20,6 +20,7 @@
 EPS = 1e-06
 
 GROUPS = FREQS // 8
+ROWS = 16
 PICK_VMEM = 58 << 20
 WHITEN_VMEM = 52 << 20
 SOURCE_VMEM = 48 << 20
@@ -55,47 +56,50 @@
     return lax.dot_general(a, b, (((1,), (0,)), ((), ())), preferred_element_type=jnp.float32)
 
 
-def pick_body(index_ref, block_ref, raw_ref, out_ref, chan_ref, sel_ref, held_ref, got_ref, sems, out_sems):
+def pick_body(index_ref, block_ref, raw_ref, out_ref, chan_ref, held_ref, got_ref, zero_ref, sems, out_sems):
     segs, count, _ = raw_ref.shape
-    parts = sems.shape[0]
-    size = segs // parts
-    copies = []
-    for i in range(parts):
-        at = pl.ds(i * size, size)
-        copies.append(pltpu.make_async_copy(raw_ref.at[at], held_ref.at[at], sems.at[i]))
-        copies[-1].start()
     first = lax.axis_index("ch") * count
     for s in range(SOURCES):
         rank = jnp.int32(0)
         for t in range(s):
             rank += jnp.where(block_ref[t] == block_ref[s], 1, 0).astype(jnp.int32)
         chan_ref[block_ref[s] * PER_BLOCK + rank] = index_ref[s] - first
-    lane = lax.broadcasted_iota(jnp.int32, (8, count), 1)
-    sub = lax.broadcasted_iota(jnp.int32, (8, count), 0)
+
+    def ours(q):
+        return (chan_ref[q] >= 0) & (chan_ref[q] < count)
+
+    def load(q):
+        start = pl.multiple_of(jnp.clip(chan_ref[q], 0, count - 1) // ROWS * ROWS, ROWS)
+        return pltpu.make_async_copy(raw_ref.at[:, pl.ds(start, ROWS)], held_ref.at[q], sems.at[q])
+
+    def store(q, source):
+        return pltpu.make_async_copy(source, out_ref.at[q], out_sems.at[q])
+
     for q in range(SOURCES):
-        hit = jnp.where(lane == chan_ref[q], 1.0, 0.0)
-        for g in range(8):
-            sel_ref[q * 8 : q * 8 + 8, g * count : (g + 1) * count] = jnp.where(sub == g, hit, 0.0)
-    select = sel_ref[...].astype(jnp.bfloat16)
-    outs = []
-    for h in range(segs // 8):
-        total = None
-        for i in range(8 * h // size, (8 * h + 8) // size):
-            copies[i].wait()
-            rows = held_ref[i * size : (i + 1) * size].reshape(size * count, SEGLEN)
-            g = (i * size) % 8
-            term = nn_dot(select[:, g * count : (g + size) * count], rows)
-            total = term if total is None else total + term
-        got_ref[h] = total.astype(jnp.bfloat16).reshape(SOURCES, 8, SEGLEN)
-        outs.append(pltpu.make_async_copy(got_ref.at[h], out_ref.at[:, h], out_sems.at[h]))
-        outs[-1].start()
-    for copy in outs:
-        copy.wait()
+        pl.when(ours(q))(lambda q=q: load(q).start())
+    zero_ref[...] = jnp.zeros_like(zero_ref)
+    for q in range(SOURCES):
+        pl.when(jnp.logical_not(ours(q)))(lambda q=q: store(q, zero_ref).start())
+    row = lax.broadcasted_iota(jnp.int32, (segs, segs * ROWS), 0)
+    column = lax.broadcasted_iota(jnp.int32, (segs, segs * ROWS), 1)
+    for q in range(SOURCES):
+
+        @pl.when(ours(q))
+        def _(q=q):
+            load(q).wait()
+            hit = column == row * ROWS + chan_ref[q] % ROWS
+            rows = held_ref[q].reshape(segs * ROWS, SEGLEN)
+            got = nn_dot(jnp.where(hit, 1.0, 0.0).astype(jnp.bfloat16), rows)
+            got_ref[q] = got.astype(jnp.bfloat16).reshape(segs // 8, 8, SEGLEN)
+            store(q, got_ref.at[q]).start()
+
+    for q in range(SOURCES):
+        store(q, zero_ref).wait()
 
 
 def pick(raw, source_index, source_block):
     segs, count, length = raw.shape
-    parts = 8
+    shape = (segs // 8, 8, length)
     return pl.pallas_call(
         pick_body,
         grid_spec=pltpu.PrefetchScalarGridSpec(
@@ -105,16 +109,16 @@
             out_specs=pl.BlockSpec(memory_space=pl.ANY),
             scratch_shapes=[
                 pltpu.SMEM((SOURCES,), jnp.int32),
-                pltpu.VMEM((SOURCES * 8, 8 * count), jnp.float32),
-                pltpu.VMEM(raw.shape, raw.dtype),
-                pltpu.VMEM((segs // 8, SOURCES, 8, length), raw.dtype),
-                pltpu.SemaphoreType.DMA((parts,)),
-                pltpu.SemaphoreType.DMA((segs // 8,)),
+                pltpu.VMEM((SOURCES, segs, ROWS, length), raw.dtype),
+                pltpu.VMEM((SOURCES, *shape), raw.dtype),
+                pltpu.VMEM(shape, raw.dtype),
+                pltpu.SemaphoreType.DMA((SOURCES,)),
+                pltpu.SemaphoreType.DMA((SOURCES,)),
             ],
         ),
-        out_shape=jax.ShapeDtypeStruct((SOURCES, segs // 8, 8, length), jnp.bfloat16),
+        out_shape=jax.ShapeDtypeStruct((SOURCES, *shape), jnp.bfloat16),
         compiler_params=pltpu.CompilerParams(vmem_limit_bytes=PICK_VMEM),
-        cost_estimate=pl.CostEstimate(flops=2 * 10**8, bytes_accessed=5 * 10**6, transcendentals=0),
+        cost_estimate=pl.CostEstimate(flops=10**8, bytes_accessed=3 * 10**6, transcendentals=0),
         name="pick",
     )(source_index, source_block, raw)
 
@@ -267,7 +271,7 @@
     lane = lax.broadcasted_iota(jnp.int32, (8, 128), 1)
     diagonal = (lane % 8) == sub
 
-    def chunk(i, carry):
+    def chunk(i):
         load(i, 0).wait()
         load(i, 1).wait()
         for j in range(blocks):
@@ -278,21 +282,21 @@
                 for h in range(2):
                     pieces = []
                     for r in range(2):
-                        row = jnp.broadcast_to(s_ref[r, 2 * q + h, pl.ds(b, 1), :], (8, 128))
+                        row = jnp.broadcast_to(s_ref[r, 2 * q + h, b : b + 1, :], (8, 128))
                         pieces.append(jnp.where(diagonal, row, 0.0))
                     halves.append(jnp.concatenate(pieces, axis=0).astype(jnp.bfloat16))
                 tiles.append(jnp.concatenate(halves, axis=1))
             cross = nn_dot(jnp.concatenate(tiles, axis=0), w_ref[b])
             high = cross.astype(jnp.bfloat16)
             low = (cross - high.astype(jnp.float32)).astype(jnp.bfloat16)
-            at = pl.ds(pl.multiple_of(b * 16, 16), 16)
+            at = slice(b * 16, b * 16 + 16)
             for q in range(SOURCES):
                 cols = slice((q % 2) * count, (q % 2 + 1) * count)
                 high_ref[q // 2, at, cols] = high[q * 16 : q * 16 + 16]
                 low_ref[q // 2, at, cols] = low[q * 16 : q * 16 + 16]
-        return carry
-
-    lax.fori_loop(0, parts, chunk, 0)
+
+    for i in range(parts):
+        chunk(i)
     table_copy.wait()
     me = lax.axis_index("seg")
     share = count // 4

time: 60.3 us -> 58.4 us (0.968)
  Pallas kernels: 28.8 us -> 27.8 us
  transfers between devices with their start and end apart: 5 -> 5, of which waited for: 4 -> 4; matrix products, arithmetic and copies ran while one was open for 0% -> 0% of each run, Pallas kernels for 25% -> 26%
where the time goes in v4:
time: 58.4 us
  Pallas kernels  27.8 us (48%)
  starting transfers between devices  19.1 us (33%)
  waiting for transfers between devices  11.5 us (20%)
    pallas_call x2, Pallas kernels, whiten(): pl.pallas_call(whiten_body, grid=(pairs,), in_specs=[pl.BlockSpec((2, cou...  14.9 us
    all_to_all x1, starting transfers between devices, local(): parts = lax.all_to_all(picked.reshape(ways, 8, SEGLEN), 'ch', 0, 0)  9.48 us
    pallas_call x1, Pallas kernels, correlate(): pl.pallas_call(correlate_body, in_specs=[vmem, anywhere, anywhere, anywhe...  6.65 us
    ppermute x3, starting transfers between devices, swap(): return lax.ppermute(x, 'seg', [(i, i ^ r) for i in range(4)])  5.41 us
    ppermute x3, waiting for transfers between devices, swap(): return lax.ppermute(x, 'seg', [(i, i ^ r) for i in range(4)])  4.84 us
    all_to_all x1, starting transfers between devices, local(): src = lax.all_to_all(spread, 'ch', 0, 0)  4.17 us
    all_to_all x1, waiting for transfers between devices, local(): parts = lax.all_to_all(picked.reshape(ways, 8, SEGLEN), 'ch', 0, 0)  3.56 us
    pallas_call x1, Pallas kernels, pick(): pl.pallas_call(pick_body, grid_spec=pltpu.PrefetchScalarGridSpec(num_scal...  3.33 us
  transfers between devices with their start and end apart: 5, of which 4 were waited for; matrix products, arithmetic and copies ran while one was open for 0% of the time, Pallas kernels for 26%

profile of v4, /device:TPU:1, one launch (start us, length us, event | category | flops | bytes accessed | tf_op | source)
XLA Modules:
  0.0 58.4 jit_solution(9905953982047187748)
XLA Ops:
  0.0 3.3 %pick.1 = bf16[16,2,8,1024]{3,2,1,0:T(8,128)(2,1)} custom-call(s32[16]{0:T(128)} %index_ref.1, s32[16]{0:T(128)} %block_ref.1, bf16[16,128,1024]{2,1,0:T(8,128)(2,1)} %raw_ref.5), custom_call_target="tpu_custom_call" | custom-call | flops 100000000 | bytes 3000000 | tf_op jit(solution)/shard_map/pick/pallas_call | solution.py:103
  3.3 9.5 %all-to-all-start = ((bf16[32,8,1024]{2,1,0:T(8,128)(2,1)}), bf16[32,8,1024]{2,1,0:T(8,128)(2,1)S(1)}, u32[]{:S(2)}, u32[]{:S(2)}) async-start(bf16[32,8,1024]{2,1,0:T(8,128)(2,1)} %bitcast.3), calls=%async_computation | async-start | bytes 1048576 | tf_op jit(solution)/shard_map/all_to_all | solution.py:386
  12.8 0.0 copy-start
  12.8 7.5 %whiten0.1 = (bf16[64,2,4,16,128]{4,3,2,1,0:T(8,128)(2,1)}, f32[8,128]{1,0:T(8,128)S(1)}) custom-call(bf16[16,128,1024]{2,1,0:T(8,128)(2,1)} %raw_ref.5, bf16[1024,1024]{1,0:T(8,128)(2,1)} %constant.4.clone.table_ref), custom_call_target="tpu_custom_call" | custom-call | flops 2147483648 | bytes 6000000 | tf_op jit(solution)/shard_map/whiten0/pallas_call | solution.py:214
  20.4 3.6 %all-to-all-done.parts_ref = bf16[32,8,1024]{2,1,0:T(8,128)(2,1)S(1)} async-done(((bf16[32,8,1024]{2,1,0:T(8,128)(2,1)}), bf16[32,8,1024]{2,1,0:T(8,128)(2,1)S(1)}, u32[]{:S(2)}, u32[]{:S(2)}) %all-to-all-start) | async-done | bytes 524320 | tf_op jit(solution)/shard_map/all_to_all | solution.py:386
  23.9 0.0 copy-done
  23.9 1.9 %source_rows.1 = bf16[32,64,128]{2,1,0:T(8,128)(2,1)} custom-call(bf16[32,8,1024]{2,1,0:T(8,128)(2,1)S(1)} %all-to-all-done.parts_ref, bf16[1024,1024]{1,0:T(8,128)(2,1)S(1)} %copy-done, f32[8,128]{1,0:T(8,128)S(1)} %get-tuple-element.12.after_ref), custom_call_target="tpu_custom_call" | custom-call | flops 16777216 | bytes 3000000 | tf_op jit(solution)/shard_map/source_rows/pallas_call | solution.py:167
  25.9 4.2 %all-to-all-start.1 = ((bf16[32,64,128]{2,1,0:T(8,128)(2,1)}), bf16[32,64,128]{2,1,0:T(8,128)(2,1)S(1)}, u32[]{:S(2)}, u32[]{:S(2)}) async-start(bf16[32,64,128]{2,1,0:T(8,128)(2,1)} %source_rows.1), calls=%async_computation.1 | async-start | bytes 1048576 | tf_op jit(solution)/shard_map/all_to_all | solution.py:389
  30.1 7.4 %whiten1.1 = (bf16[64,2,4,16,128]{4,3,2,1,0:T(8,128)(2,1)}, f32[8,128]{1,0:T(8,128)}) custom-call(bf16[16,128,1024]{2,1,0:T(8,128)(2,1)} %raw_ref.5, bf16[1024,1024]{1,0:T(8,128)(2,1)} %constant.4.clone.table_ref), custom_call_target="tpu_custom_call" | custom-call | flops 2147483648 | bytes 6000000 | tf_op jit(solution)/shard_map/whiten1/pallas_call | solution.py:214
  37.5 3.2 %all-to-all-done.1.src_ref = bf16[32,64,128]{2,1,0:T(8,128)(2,1)S(1)} async-done(((bf16[32,64,128]{2,1,0:T(8,128)(2,1)}), bf16[32,64,128]{2,1,0:T(8,128)(2,1)S(1)}, u32[]{:S(2)}, u32[]{:S(2)}) %all-to-all-start.1) | async-done | bytes 524320 | tf_op jit(solution)/shard_map/all_to_all | solution.py:389
  40.6 6.6 %correlate.1 = (f32[16,32,128]{2,1,0:T(8,128)S(1)}, f32[16,32,128]{2,1,0:T(8,128)S(1)}, f32[16,32,128]{2,1,0:T(8,128)S(1)}, f32[16,32,128]{2,1,0:T(8,128)S(1)}) custom-call(bf16[32,64,128]{2,1,0:T(8,128)(2,1)S(1)} %all-to-all-done.1.src_ref, bf16[64,128,128]{2,1,0:T(8,128)(2,1)} %bitcast.4, bf16[64,128,128]{2,1,0:T(8,128)(2,1)} %bitcast.5, ...), custom_call_target="tpu_custom_call" | custom-call | flops 3000000000 | bytes 6000000 | tf_op jit(solution)/shard_map/correlate/pallas_call | solution.py:324
  47.3 2.8 %collective-permute-start.1 = (f32[16,32,128]{2,1,0:T(8,128)S(1)}, f32[16,32,128]{2,1,0:T(8,128)S(1)}, u32[]{:S(2)}, u32[]{:S(2)}) collective-permute-start(f32[16,32,128]{2,1,0:T(8,128)S(1)} %get-tuple-element.18), channel_id=1, source_target_pairs={{0,32},{32,0},{64,96},{96,64},{1,33},{33,1},{65,97},{97,65},{2,34}... | collective-permute-start | bytes 786440 | tf_op jit(solution)/shard_map/ppermute | solution.py:394
  50.1 0.1 collective-permute-start
  50.2 1.1 %collective-permute-done.1.core_ref = f32[16,32,128]{2,1,0:T(8,128)S(1)} collective-permute-done((f32[16,32,128]{2,1,0:T(8,128)S(1)}, f32[16,32,128]{2,1,0:T(8,128)S(1)}, u32[]{:S(2)}, u32[]{:S(2)}) %collective-permute-start.1) | collective-permute-done | bytes 262176 | tf_op jit(solution)/shard_map/ppermute | solution.py:394
  51.3 2.5 %collective-permute-start.2 = (bf16[16,32,128]{2,1,0:T(8,128)(2,1)S(1)}, bf16[16,32,128]{2,1,0:T(8,128)(2,1)S(1)}, u32[]{:S(2)}, u32[]{:S(2)}) collective-permute-start(bf16[16,32,128]{2,1,0:T(8,128)(2,1)S(1)} %chip_sum.1), channel_id=1, source_target_pairs={{0,64},{32,96},{64,0},{96,32},{1,65},{33,97},{65,1},{97,33},{2,66}... | collective-permute-start | bytes 393224 | tf_op jit(solution)/shard_map/ppermute | solution.py:394
  53.8 0.0 collective-permute-done.core_ref
  53.8 3.8 %collective-permute-done.2.far_ref = bf16[16,32,128]{2,1,0:T(8,128)(2,1)S(1)} collective-permute-done((bf16[16,32,128]{2,1,0:T(8,128)(2,1)S(1)}, bf16[16,32,128]{2,1,0:T(8,128)(2,1)S(1)}, u32[]{:S(2)}, u32[]{:S(2)}) %collective-permute-start.2) | collective-permute-done | bytes 131104 | tf_op jit(solution)/shard_map/ppermute | solution.py:394
  57.6 0.9 %gather_sum.1 = f32[32,16,128]{2,1,0:T(8,128)} custom-call(f32[16,32,128]{2,1,0:T(8,128)S(1)} %get-tuple-element.15.mine_ref, f32[16,32,128]{2,1,0:T(8,128)S(1)} %collective-permute-done.core_ref, bf16[16,32,128]{2,1,0:T(8,128)(2,1)S(1)} %collective-permute-done.2.far_ref), custom_call_target="tpu_custom_call" | custom-call | flops 1000000 | bytes 1000000 | tf_op jit(solution)/shard_map/gather_sum/pallas_call | solution.py:369
  (1 shorter events, 0.0 us)
Async XLA Ops:
  3.3 20.6 %all-to-all-start = ((bf16[32,8,1024]{2,1,0:T(8,128)(2,1)}), bf16[32,8,1024]{2,1,0:T(8,128)(2,1)S(1)}, u32[]{:S(2)}, u32[]{:S(2)}) async-start(bf16[32,8,1024]{2,1,0:T(8,128)(2,1)} %bitcast.3), calls=%async_computation | async-start | bytes 1048576 | tf_op jit(solution)/shard_map/all_to_all | solution.py:386
  12.8 11.1 %copy-start = (bf16[1024,1024]{1,0:T(8,128)(2,1)S(1)}, bf16[1024,1024]{1,0:T(8,128)(2,1)}, u32[]{:S(2)}) copy-start(bf16[1024,1024]{1,0:T(8,128)(2,1)} %constant.4.clone.table_ref) | copy-start | bytes 6291460
  25.9 14.7 %all-to-all-start.1 = ((bf16[32,64,128]{2,1,0:T(8,128)(2,1)}), bf16[32,64,128]{2,1,0:T(8,128)(2,1)S(1)}, u32[]{:S(2)}, u32[]{:S(2)}) async-start(bf16[32,64,128]{2,1,0:T(8,128)(2,1)} %source_rows.1), calls=%async_computation.1 | async-start | bytes 1048576 | tf_op jit(solution)/shard_map/all_to_all | solution.py:389
  47.3 4.0 %collective-permute-start.1 = (f32[16,32,128]{2,1,0:T(8,128)S(1)}, f32[16,32,128]{2,1,0:T(8,128)S(1)}, u32[]{:S(2)}, u32[]{:S(2)}) collective-permute-start(f32[16,32,128]{2,1,0:T(8,128)S(1)} %get-tuple-element.18), channel_id=1, source_target_pairs={{0,32},{32,0},{64,96},{96,64},{1,33},{33,1},{65,97},{97,65},{2,34}... | collective-permute-start | bytes 786440 | tf_op jit(solution)/shard_map/ppermute | solution.py:394
  50.1 3.7 %collective-permute-start = (f32[16,32,128]{2,1,0:T(8,128)S(1)}, f32[16,32,128]{2,1,0:T(8,128)S(1)}, u32[]{:S(2)}, u32[]{:S(2)}) collective-permute-start(f32[16,32,128]{2,1,0:T(8,128)S(1)} %get-tuple-element.16), channel_id=1, source_target_pairs={{0,32},{32,0},{64,96},{96,64},{1,33},{33,1},{65,97},{97,65},{2,34}... | collective-permute-start | bytes 786440 | tf_op jit(solution)/shard_map/ppermute | solution.py:394
  51.3 6.3 %collective-permute-start.2 = (bf16[16,32,128]{2,1,0:T(8,128)(2,1)S(1)}, bf16[16,32,128]{2,1,0:T(8,128)(2,1)S(1)}, u32[]{:S(2)}, u32[]{:S(2)}) collective-permute-start(bf16[16,32,128]{2,1,0:T(8,128)(2,1)S(1)} %chip_sum.1), channel_id=1, source_target_pairs={{0,64},{32,96},{64,0},{96,32},{1,65},{33,97},{65,1},{97,33},{2,66}... | collective-permute-start | bytes 393224 | tf_op jit(solution)/shard_map/ppermute | solution.py:394

commit v5 on v4

--- a/solution.py
+++ b/solution.py
@@ -21,6 +21,7 @@
 
 GROUPS = FREQS // 8
 ROWS = 16
+PARTS = (0, 8, 32, 64)
 PICK_VMEM = 58 << 20
 WHITEN_VMEM = 52 << 20
 SOURCE_VMEM = 48 << 20
@@ -175,13 +176,19 @@
     )(parts, table, after)
 
 
-def whiten_body(raw_ref, table_ref, out_ref, done_ref, spec_ref, amp_ref):
+def whiten_body(raw_ref, half_ref, out_ref, done_ref, spec_ref, amp_ref, table_ref):
+    @pl.when(pl.program_id(0) == 0)
+    def _():
+        row = lax.broadcasted_iota(jnp.int32, half_ref.shape, 0)
+        part = half_ref[...]
+        table_ref[:, : SEGLEN // 2] = part
+        table_ref[:, SEGLEN // 2 :] = jnp.where(row % 2 == 0, -part, part)
+
     count = raw_ref.shape[1]
     width = 2 * count
     step = 32
     size = step + 16
     zero = jnp.zeros((8, width), jnp.float32)
-    done_ref[...] = zero[:, :128]
     amp_ref[0:8, :] = zero
     amp_ref[FREQS + 8 : FREQS + 16, :] = zero
     spec_ref[...] = nt_dot(table_ref[...], raw_ref[...].reshape(width, SEGLEN))
@@ -216,11 +223,11 @@
         grid=(pairs,),
         in_specs=[
             pl.BlockSpec((2, count, length), lambda i: (i + half * pairs, 0, 0)),
-            pl.BlockSpec((2 * FREQS, length), lambda i: (0, 0)),
+            pl.BlockSpec((2 * FREQS, length // 2), lambda i: (0, 0)),
         ],
         out_specs=[
             pl.BlockSpec((GROUPS, 2, 1, 16, count), lambda i: (0, 0, i, 0, 0)),
-            pl.BlockSpec((8, 128), lambda i: (0, 0)),
+            pl.BlockSpec(memory_space=pl.ANY),
         ],
         out_shape=[
             jax.ShapeDtypeStruct((GROUPS, 2, pairs, 16, count), jnp.bfloat16),
@@ -229,6 +236,7 @@
         scratch_shapes=[
             pltpu.VMEM((2 * FREQS, 2 * count), jnp.float32),
             pltpu.VMEM((FREQS + 16, 2 * count), jnp.float32),
+            pltpu.VMEM((2 * FREQS, length), jnp.bfloat16),
         ],
         compiler_params=pltpu.CompilerParams(vmem_limit_bytes=WHITEN_VMEM),
         cost_estimate=pl.CostEstimate(
@@ -244,11 +252,10 @@
     s_ref, w_ref, table_ref, high_ref, low_ref, sum_ref, sems, table_sem = refs[4:]
     count = w0_ref.shape[2]
     deep = w0_ref.shape[1]
-    parts = sems.shape[0]
-    blocks = GROUPS // parts
+    parts = len(PARTS) - 1
 
     def load(i, half):
-        at = pl.ds(i * blocks, blocks)
+        at = pl.ds(PARTS[i], PARTS[i + 1] - PARTS[i])
         source = (w0_ref, w1_ref)[half]
         return pltpu.make_async_copy(
             source.at[at], w_ref.at[at, pl.ds(half * deep, deep)], sems.at[i, half]
@@ -274,8 +281,7 @@
     def chunk(i):
         load(i, 0).wait()
         load(i, 1).wait()
-        for j in range(blocks):
-            b = i * blocks + j
+        for b in range(PARTS[i], PARTS[i + 1]):
             tiles = []
             for q in range(SOURCES):
                 halves = []
@@ -316,7 +322,7 @@
 
 def correlate(src, w0, w1, lag):
     count = w0.shape[2]
-    parts = 8
+    parts = len(PARTS) - 1
     share = count // 4
     shape = (SOURCES, share, LAGS)
     vmem = pl.BlockSpec(memory_space=pltpu.VMEM)

time: 58.4 us -> 57.6 us (0.986); the launches traced: 58.4 us -> 56.8 us
  Pallas kernels: 27.8 us -> 26.9 us
  starting transfers between devices: 19.1 us -> 18.3 us
    all_to_all x1, starting transfers between devices: 9.48 us -> 8.56 us  [local(): parts = lax.all_to_all(picked.reshape(ways, 8, SEGLEN), 'ch', 0, 0)]
    pallas_call x1, Pallas kernels: 6.65 us -> 5.86 us  [correlate(): pl.pallas_call(correlate_body, in_specs=[vmem, anywhere, anywhere, anywhe...]
where the time goes in v5:
time: 57.6 us; the launch traced here: 56.8 us
  Pallas kernels  26.9 us (47%)
  starting transfers between devices  18.3 us (32%)
  waiting for transfers between devices  11.5 us (20%)
    pallas_call x2, Pallas kernels, whiten(): pl.pallas_call(whiten_body, grid=(pairs,), in_specs=[pl.BlockSpec((2, cou...  14.7 us
    all_to_all x1, starting transfers between devices, local(): parts = lax.all_to_all(picked.reshape(ways, 8, SEGLEN), 'ch', 0, 0)  8.56 us
    pallas_call x1, Pallas kernels, correlate(): pl.pallas_call(correlate_body, in_specs=[vmem, anywhere, anywhere, anywhe...  5.86 us
    ppermute x3, starting transfers between devices, swap(): return lax.ppermute(x, 'seg', [(i, i ^ r) for i in range(4)])  5.71 us
    ppermute x3, waiting for transfers between devices, swap(): return lax.ppermute(x, 'seg', [(i, i ^ r) for i in range(4)])  4.54 us
    all_to_all x1, starting transfers between devices, local(): src = lax.all_to_all(spread, 'ch', 0, 0)  4.06 us
    all_to_all x1, waiting for transfers between devices, local(): parts = lax.all_to_all(picked.reshape(ways, 8, SEGLEN), 'ch', 0, 0)  3.67 us
    pallas_call x1, Pallas kernels, pick(): pl.pallas_call(pick_body, grid_spec=pltpu.PrefetchScalarGridSpec(num_scal...  3.49 us
  transfers between devices with their start and end apart: 5, of which 4 were waited for; matrix products, arithmetic and copies ran while one was open for 0% of the time, Pallas kernels for 26%

profile of v5, /device:TPU:1, one launch (start us, length us, event | category | flops | bytes accessed | tf_op | source)
XLA Modules:
  0.0 56.8 jit_solution(576628426310857255)
XLA Ops:
  0.0 3.5 %pick.1 = bf16[16,2,8,1024]{3,2,1,0:T(8,128)(2,1)} custom-call(s32[16]{0:T(128)} %index_ref.1, s32[16]{0:T(128)} %block_ref.1, bf16[16,128,1024]{2,1,0:T(8,128)(2,1)} %raw_ref.5), custom_call_target="tpu_custom_call" | custom-call | flops 100000000 | bytes 3000000 | tf_op jit(solution)/shard_map/pick/pallas_call | solution.py:104
  3.5 8.6 %all-to-all-start = ((bf16[32,8,1024]{2,1,0:T(8,128)(2,1)}), bf16[32,8,1024]{2,1,0:T(8,128)(2,1)S(1)}, u32[]{:S(2)}, u32[]{:S(2)}) async-start(bf16[32,8,1024]{2,1,0:T(8,128)(2,1)} %bitcast.3), calls=%async_computation | async-start | bytes 1048576 | tf_op jit(solution)/shard_map/all_to_all | solution.py:392
  12.1 0.0 copy-start
  12.1 7.4 %whiten0.1 = (bf16[64,2,4,16,128]{4,3,2,1,0:T(8,128)(2,1)}, f32[8,128]{1,0:T(8,128)S(1)}) custom-call(bf16[16,128,1024]{2,1,0:T(8,128)(2,1)} %raw_ref.5, bf16[1024,1024]{1,0:T(8,128)(2,1)} %constant.4.clone.half_ref.table_ref), custom_call_target="tpu_custom_call" | custom-call | flops 2147483648 | bytes 6000000 | tf_op jit(solution)/shard_map/whiten0/pallas_call | solution.py:221
  19.5 3.7 %all-to-all-done.parts_ref = bf16[32,8,1024]{2,1,0:T(8,128)(2,1)S(1)} async-done(((bf16[32,8,1024]{2,1,0:T(8,128)(2,1)}), bf16[32,8,1024]{2,1,0:T(8,128)(2,1)S(1)}, u32[]{:S(2)}, u32[]{:S(2)}) %all-to-all-start) | async-done | bytes 524320 | tf_op jit(solution)/shard_map/all_to_all | solution.py:392
  23.2 0.0 copy-done
  23.2 1.9 %source_rows.1 = bf16[32,64,128]{2,1,0:T(8,128)(2,1)} custom-call(bf16[32,8,1024]{2,1,0:T(8,128)(2,1)S(1)} %all-to-all-done.parts_ref, bf16[1024,1024]{1,0:T(8,128)(2,1)S(1)} %copy-done, f32[8,128]{1,0:T(8,128)S(1)} %get-tuple-element.12.after_ref), custom_call_target="tpu_custom_call" | custom-call | flops 16777216 | bytes 3000000 | tf_op jit(solution)/shard_map/source_rows/pallas_call | solution.py:168
  25.1 4.1 %all-to-all-start.1 = ((bf16[32,64,128]{2,1,0:T(8,128)(2,1)}), bf16[32,64,128]{2,1,0:T(8,128)(2,1)S(1)}, u32[]{:S(2)}, u32[]{:S(2)}) async-start(bf16[32,64,128]{2,1,0:T(8,128)(2,1)} %source_rows.1), calls=%async_computation.1 | async-start | bytes 1048576 | tf_op jit(solution)/shard_map/all_to_all | solution.py:395
  29.2 7.3 %whiten1.1 = (bf16[64,2,4,16,128]{4,3,2,1,0:T(8,128)(2,1)}, f32[8,128]{1,0:T(8,128)}) custom-call(bf16[16,128,1024]{2,1,0:T(8,128)(2,1)} %raw_ref.5, bf16[1024,1024]{1,0:T(8,128)(2,1)} %constant.4.clone.half_ref.table_ref), custom_call_target="tpu_custom_call" | custom-call | flops 2147483648 | bytes 6000000 | tf_op jit(solution)/shard_map/whiten1/pallas_call | solution.py:221
  36.5 3.3 %all-to-all-done.1.src_ref = bf16[32,64,128]{2,1,0:T(8,128)(2,1)S(1)} async-done(((bf16[32,64,128]{2,1,0:T(8,128)(2,1)}), bf16[32,64,128]{2,1,0:T(8,128)(2,1)S(1)}, u32[]{:S(2)}, u32[]{:S(2)}) %all-to-all-start.1) | async-done | bytes 524320 | tf_op jit(solution)/shard_map/all_to_all | solution.py:395
  39.7 5.9 %correlate.1 = (f32[16,32,128]{2,1,0:T(8,128)S(1)}, f32[16,32,128]{2,1,0:T(8,128)S(1)}, f32[16,32,128]{2,1,0:T(8,128)S(1)}, f32[16,32,128]{2,1,0:T(8,128)S(1)}) custom-call(bf16[32,64,128]{2,1,0:T(8,128)(2,1)S(1)} %all-to-all-done.1.src_ref, bf16[64,128,128]{2,1,0:T(8,128)(2,1)} %bitcast.4, bf16[64,128,128]{2,1,0:T(8,128)(2,1)} %bitcast.5, ...), custom_call_target="tpu_custom_call" | custom-call | flops 3000000000 | bytes 6000000 | tf_op jit(solution)/shard_map/correlate/pallas_call | solution.py:330
  45.6 2.8 %collective-permute-start.1 = (f32[16,32,128]{2,1,0:T(8,128)S(1)}, f32[16,32,128]{2,1,0:T(8,128)S(1)}, u32[]{:S(2)}, u32[]{:S(2)}) collective-permute-start(f32[16,32,128]{2,1,0:T(8,128)S(1)} %get-tuple-element.18), channel_id=1, source_target_pairs={{0,32},{32,0},{64,96},{96,64},{1,33},{33,1},{65,97},{97,65},{2,34}... | collective-permute-start | bytes 786440 | tf_op jit(solution)/shard_map/ppermute | solution.py:400
  48.4 0.1 collective-permute-start
  48.5 1.1 %collective-permute-done.1.core_ref = f32[16,32,128]{2,1,0:T(8,128)S(1)} collective-permute-done((f32[16,32,128]{2,1,0:T(8,128)S(1)}, f32[16,32,128]{2,1,0:T(8,128)S(1)}, u32[]{:S(2)}, u32[]{:S(2)}) %collective-permute-start.1) | collective-permute-done | bytes 262176 | tf_op jit(solution)/shard_map/ppermute | solution.py:400
  49.6 2.8 %collective-permute-start.2 = (bf16[16,32,128]{2,1,0:T(8,128)(2,1)S(1)}, bf16[16,32,128]{2,1,0:T(8,128)(2,1)S(1)}, u32[]{:S(2)}, u32[]{:S(2)}) collective-permute-start(bf16[16,32,128]{2,1,0:T(8,128)(2,1)S(1)} %chip_sum.1), channel_id=1, source_target_pairs={{0,64},{32,96},{64,0},{96,32},{1,65},{33,97},{65,1},{97,33},{2,66}... | collective-permute-start | bytes 393224 | tf_op jit(solution)/shard_map/ppermute | solution.py:400
  52.4 0.0 collective-permute-done.core_ref
  52.4 3.5 %collective-permute-done.2.far_ref = bf16[16,32,128]{2,1,0:T(8,128)(2,1)S(1)} collective-permute-done((bf16[16,32,128]{2,1,0:T(8,128)(2,1)S(1)}, bf16[16,32,128]{2,1,0:T(8,128)(2,1)S(1)}, u32[]{:S(2)}, u32[]{:S(2)}) %collective-permute-start.2) | collective-permute-done | bytes 131104 | tf_op jit(solution)/shard_map/ppermute | solution.py:400
  55.9 0.9 %gather_sum.1 = f32[32,16,128]{2,1,0:T(8,128)} custom-call(f32[16,32,128]{2,1,0:T(8,128)S(1)} %get-tuple-element.15.mine_ref, f32[16,32,128]{2,1,0:T(8,128)S(1)} %collective-permute-done.core_ref, bf16[16,32,128]{2,1,0:T(8,128)(2,1)S(1)} %collective-permute-done.2.far_ref), custom_call_target="tpu_custom_call" | custom-call | flops 1000000 | bytes 1000000 | tf_op jit(solution)/shard_map/gather_sum/pallas_call | solution.py:375
  (1 shorter events, 0.0 us)
Async XLA Ops:
  3.5 19.7 %all-to-all-start = ((bf16[32,8,1024]{2,1,0:T(8,128)(2,1)}), bf16[32,8,1024]{2,1,0:T(8,128)(2,1)S(1)}, u32[]{:S(2)}, u32[]{:S(2)}) async-start(bf16[32,8,1024]{2,1,0:T(8,128)(2,1)} %bitcast.3), calls=%async_computation | async-start | bytes 1048576 | tf_op jit(solution)/shard_map/all_to_all | solution.py:392
  12.1 11.1 %copy-start = (bf16[1024,1024]{1,0:T(8,128)(2,1)S(1)}, bf16[1024,1024]{1,0:T(8,128)(2,1)}, u32[]{:S(2)}) copy-start(bf16[1024,1024]{1,0:T(8,128)(2,1)} %constant.4.clone.half_ref.table_ref) | copy-start | bytes 6291460
  25.1 14.6 %all-to-all-start.1 = ((bf16[32,64,128]{2,1,0:T(8,128)(2,1)}), bf16[32,64,128]{2,1,0:T(8,128)(2,1)S(1)}, u32[]{:S(2)}, u32[]{:S(2)}) async-start(bf16[32,64,128]{2,1,0:T(8,128)(2,1)} %source_rows.1), calls=%async_computation.1 | async-start | bytes 1048576 | tf_op jit(solution)/shard_map/all_to_all | solution.py:395
  45.6 4.0 %collective-permute-start.1 = (f32[16,32,128]{2,1,0:T(8,128)S(1)}, f32[16,32,128]{2,1,0:T(8,128)S(1)}, u32[]{:S(2)}, u32[]{:S(2)}) collective-permute-start(f32[16,32,128]{2,1,0:T(8,128)S(1)} %get-tuple-element.18), channel_id=1, source_target_pairs={{0,32},{32,0},{64,96},{96,64},{1,33},{33,1},{65,97},{97,65},{2,34}... | collective-permute-start | bytes 786440 | tf_op jit(solution)/shard_map/ppermute | solution.py:400
  48.4 4.0 %collective-permute-start = (f32[16,32,128]{2,1,0:T(8,128)S(1)}, f32[16,32,128]{2,1,0:T(8,128)S(1)}, u32[]{:S(2)}, u32[]{:S(2)}) collective-permute-start(f32[16,32,128]{2,1,0:T(8,128)S(1)} %get-tuple-element.16), channel_id=1, source_target_pairs={{0,32},{32,0},{64,96},{96,64},{1,33},{33,1},{65,97},{97,65},{2,34}... | collective-permute-start | bytes 786440 | tf_op jit(solution)/shard_map/ppermute | solution.py:400
  49.6 6.3 %collective-permute-start.2 = (bf16[16,32,128]{2,1,0:T(8,128)(2,1)S(1)}, bf16[16,32,128]{2,1,0:T(8,128)(2,1)S(1)}, u32[]{:S(2)}, u32[]{:S(2)}) collective-permute-start(bf16[16,32,128]{2,1,0:T(8,128)(2,1)S(1)} %chip_sum.1), channel_id=1, source_target_pairs={{0,64},{32,96},{64,0},{96,32},{1,65},{33,97},{65,1},{97,33},{2,66}... | collective-permute-start | bytes 393224 | tf_op jit(solution)/shard_map/ppermute | solution.py:400

commit v6 on v5

--- a/solution.py
+++ b/solution.py
@@ -21,6 +21,7 @@
 
 GROUPS = FREQS // 8
 ROWS = 16
+LAG_ROWS = 80
 PARTS = (0, 8, 32, 64)
 PICK_VMEM = 58 << 20
 WHITEN_VMEM = 52 << 20
@@ -39,14 +40,13 @@
 
 def lag_rows(scale):
     bins = np.arange(1, FREQS + 1)[None, :]
-    lags = np.arange(LAGS)[:, None] - HALFLAG
+    lags = np.arange(LAG_ROWS)[:, None]
     theta = ((bins * lags) % SEGLEN).astype(np.float32) * np.float32(2.0 * np.pi / SEGLEN)
-    cos = np.cos(theta).reshape(LAGS, GROUPS, 1, 8)
-    sin = np.sin(theta).reshape(LAGS, GROUPS, 1, 8)
-    table = np.concatenate([cos, sin], axis=2).reshape(LAGS, 2 * FREQS) * np.float32(scale)
+    table = np.stack([np.cos(theta), np.sin(theta)]) * np.float32(scale)
+    table = np.where(lags[None] <= HALFLAG, table, np.float32(0.0)).astype(np.float32)
     high = table.astype(ml_dtypes.bfloat16)
     low = (table - high.astype(np.float32)).astype(ml_dtypes.bfloat16)
-    return np.concatenate([high, low], axis=0)
+    return np.concatenate([high, low], axis=1)
 
 
 def nt_dot(a, b):
@@ -278,28 +278,44 @@
     lane = lax.broadcasted_iota(jnp.int32, (8, 128), 1)
     diagonal = (lane % 8) == sub
 
+    def cross(b):
+        tiles = []
+        for q in range(SOURCES):
+            halves = []
+            for h in range(2):
+                pieces = []
+                for r in range(2):
+                    row = jnp.broadcast_to(s_ref[r, 2 * q + h, b : b + 1, :], (8, 128))
+                    pieces.append(jnp.where(diagonal, row, 0.0))
+                halves.append(jnp.concatenate(pieces, axis=0).astype(jnp.bfloat16))
+            tiles.append(jnp.concatenate(halves, axis=1))
+        return nn_dot(jnp.concatenate(tiles, axis=0), w_ref[b])
+
+    def turn(x):
+        x = x.reshape(LAG_ROWS // 8, 8, x.shape[1])[: HALFLAG // 8 + 1]
+        row = lax.broadcasted_iota(jnp.int32, x.shape, 1)
+        even = jnp.where(row % 4 == 0, x, pltpu.roll(x, 4, 1))
+        odd = jnp.where(row % 4 == 1, pltpu.roll(x, 2, 1), pltpu.roll(x, 6, 1))
+        x = jnp.where(row % 2 == 0, even, odd)
+        groups = []
+        for j in range(HALFLAG // 8):
+            groups.append(jnp.where(row[0] == 0, x[HALFLAG // 8 - j], x[HALFLAG // 8 - 1 - j]))
+        return jnp.concatenate(groups, axis=0)
+
     def chunk(i):
         load(i, 0).wait()
         load(i, 1).wait()
-        for b in range(PARTS[i], PARTS[i + 1]):
-            tiles = []
-            for q in range(SOURCES):
-                halves = []
-                for h in range(2):
-                    pieces = []
-                    for r in range(2):
-                        row = jnp.broadcast_to(s_ref[r, 2 * q + h, b : b + 1, :], (8, 128))
-                        pieces.append(jnp.where(diagonal, row, 0.0))
-                    halves.append(jnp.concatenate(pieces, axis=0).astype(jnp.bfloat16))
-                tiles.append(jnp.concatenate(halves, axis=1))
-            cross = nn_dot(jnp.concatenate(tiles, axis=0), w_ref[b])
-            high = cross.astype(jnp.bfloat16)
-            low = (cross - high.astype(jnp.float32)).astype(jnp.bfloat16)
-            at = slice(b * 16, b * 16 + 16)
+        for b in range(PARTS[i], PARTS[i + 1], 2):
+            one, two = cross(b), cross(b + 1)
+            at = slice(b * 8, b * 8 + 16)
             for q in range(SOURCES):
                 cols = slice((q % 2) * count, (q % 2 + 1) * count)
-                high_ref[q // 2, at, cols] = high[q * 16 : q * 16 + 16]
-                low_ref[q // 2, at, cols] = low[q * 16 : q * 16 + 16]
+                for r in range(2):
+                    rows = slice(q * 16 + r * 8, q * 16 + r * 8 + 8)
+                    both = jnp.concatenate([one[rows], two[rows]], axis=0)
+                    high = both.astype(jnp.bfloat16)
+                    high_ref[q // 2, r, at, cols] = high
+                    low_ref[q // 2, r, at, cols] = (both - high.astype(jnp.float32)).astype(jnp.bfloat16)
 
     for i in range(parts):
         chunk(i)
@@ -307,9 +323,13 @@
     me = lax.axis_index("seg")
     share = count // 4
     for p in range(SOURCES // 2):
-        first = nn_dot(table_ref[...], high_ref[p])
-        second = nn_dot(table_ref[:LAGS, :], low_ref[p])
-        total = first[:LAGS] + (first[LAGS:] + second)
+        terms = []
+        for r in range(2):
+            first = nn_dot(table_ref[r], high_ref[p, r])
+            second = nn_dot(table_ref[r, :LAG_ROWS, :], low_ref[p, r])
+            terms.append(first[:LAG_ROWS] + (first[LAG_ROWS:] + second))
+        later = terms[0][:HALFLAG] + terms[1][:HALFLAG]
+        total = jnp.concatenate([turn(terms[0] - terms[1]), later], axis=0)
         for i in range(2):
             sum_ref[2 * p + i] = total[:, i * count : (i + 1) * count].T
 
@@ -336,8 +356,8 @@
             pltpu.VMEM((2, 2 * SOURCES, GROUPS, 128), jnp.float32),
             pltpu.VMEM((GROUPS, 2 * w0.shape[1], count), jnp.bfloat16),
             pltpu.VMEM(lag.shape, lag.dtype),
-            pltpu.VMEM((SOURCES // 2, 2 * FREQS, 2 * count), jnp.bfloat16),
-            pltpu.VMEM((SOURCES // 2, 2 * FREQS, 2 * count), jnp.bfloat16),
+            pltpu.VMEM((SOURCES // 2, 2, FREQS, 2 * count), jnp.bfloat16),
+            pltpu.VMEM((SOURCES // 2, 2, FREQS, 2 * count), jnp.bfloat16),
             pltpu.VMEM((SOURCES, count, LAGS), jnp.float32),
             pltpu.SemaphoreType.DMA((parts, 2)),
             pltpu.SemaphoreType.DMA,

time: 57.6 us -> 57.7 us (level)
  starting transfers between devices: 18.3 us -> 20.4 us
  Pallas kernels: 26.9 us -> 25 us
    all_to_all x1, starting transfers between devices: 8.56 us -> 10.9 us  [local(): parts = lax.all_to_all(picked.reshape(ways, 8, SEGLEN), 'ch', 0, 0)]
    pallas_call x1, Pallas kernels: 3.49 us -> 1.92 us  [pick(): pl.pallas_call(pick_body, grid_spec=pltpu.PrefetchScalarGridSpec(num_scal...]
where the time goes in v6:
time: 57.7 us; the launch traced here: 57.2 us
  Pallas kernels  25 us (43%)
  starting transfers between devices  20.4 us (35%)
  waiting for transfers between devices  11.7 us (20%)
    pallas_call x2, Pallas kernels, whiten(): pl.pallas_call(whiten_body, grid=(pairs,), in_specs=[pl.BlockSpec((2, cou...  14.7 us
    all_to_all x1, starting transfers between devices, local(): parts = lax.all_to_all(picked.reshape(ways, 8, SEGLEN), 'ch', 0, 0)  10.9 us
    pallas_call x1, Pallas kernels, correlate(): pl.pallas_call(correlate_body, in_specs=[vmem, anywhere, anywhere, anywhe...  5.56 us
    ppermute x3, starting transfers between devices, swap(): return lax.ppermute(x, 'seg', [(i, i ^ r) for i in range(4)])  5.45 us
    ppermute x3, waiting for transfers between devices, swap(): return lax.ppermute(x, 'seg', [(i, i ^ r) for i in range(4)])  4.82 us
    all_to_all x1, starting transfers between devices, local(): src = lax.all_to_all(spread, 'ch', 0, 0)  4.05 us
    all_to_all x1, waiting for transfers between devices, local(): parts = lax.all_to_all(picked.reshape(ways, 8, SEGLEN), 'ch', 0, 0)  3.67 us
    all_to_all x1, waiting for transfers between devices, local(): src = lax.all_to_all(spread, 'ch', 0, 0)  3.21 us
  transfers between devices with their start and end apart: 5, of which 4 were waited for; matrix products, arithmetic and copies ran while one was open for 0% of the time, Pallas kernels for 26%

profile of v6, /device:TPU:1, one launch (start us, length us, event | category | flops | bytes accessed | tf_op | source)
XLA Modules:
  0.0 57.2 jit_solution(13657165217391389080)
XLA Ops:
  0.0 1.9 %pick.1 = bf16[16,2,8,1024]{3,2,1,0:T(8,128)(2,1)} custom-call(s32[16]{0:T(128)} %index_ref.1, s32[16]{0:T(128)} %block_ref.1, bf16[16,128,1024]{2,1,0:T(8,128)(2,1)} %raw_ref.5), custom_call_target="tpu_custom_call" | custom-call | flops 100000000 | bytes 3000000 | tf_op jit(solution)/shard_map/pick/pallas_call | solution.py:104
  1.9 10.9 %all-to-all-start = ((bf16[32,8,1024]{2,1,0:T(8,128)(2,1)}), bf16[32,8,1024]{2,1,0:T(8,128)(2,1)S(1)}, u32[]{:S(2)}, u32[]{:S(2)}) async-start(bf16[32,8,1024]{2,1,0:T(8,128)(2,1)} %bitcast.3), calls=%async_computation | async-start | bytes 1048576 | tf_op jit(solution)/shard_map/all_to_all | solution.py:412
  12.8 0.0 copy-start
  12.8 7.4 %whiten0.1 = (bf16[64,2,4,16,128]{4,3,2,1,0:T(8,128)(2,1)}, f32[8,128]{1,0:T(8,128)S(1)}) custom-call(bf16[16,128,1024]{2,1,0:T(8,128)(2,1)} %raw_ref.5, bf16[1024,1024]{1,0:T(8,128)(2,1)} %constant.4.clone.half_ref.table_ref), custom_call_target="tpu_custom_call" | custom-call | flops 2147483648 | bytes 6000000 | tf_op jit(solution)/shard_map/whiten0/pallas_call | solution.py:221
  20.3 3.7 %all-to-all-done.parts_ref = bf16[32,8,1024]{2,1,0:T(8,128)(2,1)S(1)} async-done(((bf16[32,8,1024]{2,1,0:T(8,128)(2,1)}), bf16[32,8,1024]{2,1,0:T(8,128)(2,1)S(1)}, u32[]{:S(2)}, u32[]{:S(2)}) %all-to-all-start) | async-done | bytes 524320 | tf_op jit(solution)/shard_map/all_to_all | solution.py:412
  23.9 0.0 copy-done
  23.9 1.9 %source_rows.1 = bf16[32,64,128]{2,1,0:T(8,128)(2,1)} custom-call(bf16[32,8,1024]{2,1,0:T(8,128)(2,1)S(1)} %all-to-all-done.parts_ref, bf16[1024,1024]{1,0:T(8,128)(2,1)S(1)} %copy-done, f32[8,128]{1,0:T(8,128)S(1)} %get-tuple-element.12.after_ref), custom_call_target="tpu_custom_call" | custom-call | flops 16777216 | bytes 3000000 | tf_op jit(solution)/shard_map/source_rows/pallas_call | solution.py:168
  25.9 4.1 %all-to-all-start.1 = ((bf16[32,64,128]{2,1,0:T(8,128)(2,1)}), bf16[32,64,128]{2,1,0:T(8,128)(2,1)S(1)}, u32[]{:S(2)}, u32[]{:S(2)}) async-start(bf16[32,64,128]{2,1,0:T(8,128)(2,1)} %source_rows.1), calls=%async_computation.1 | async-start | bytes 1048576 | tf_op jit(solution)/shard_map/all_to_all | solution.py:415
  29.9 0.0 copy-start.1
  29.9 7.3 %whiten1.1 = (bf16[64,2,4,16,128]{4,3,2,1,0:T(8,128)(2,1)}, f32[8,128]{1,0:T(8,128)}) custom-call(bf16[16,128,1024]{2,1,0:T(8,128)(2,1)} %raw_ref.5, bf16[1024,1024]{1,0:T(8,128)(2,1)} %constant.4.clone.half_ref.table_ref), custom_call_target="tpu_custom_call" | custom-call | flops 2147483648 | bytes 6000000 | tf_op jit(solution)/shard_map/whiten1/pallas_call | solution.py:221
  37.3 3.2 %all-to-all-done.1.src_ref = bf16[32,64,128]{2,1,0:T(8,128)(2,1)S(1)} async-done(((bf16[32,64,128]{2,1,0:T(8,128)(2,1)}), bf16[32,64,128]{2,1,0:T(8,128)(2,1)S(1)}, u32[]{:S(2)}, u32[]{:S(2)}) %all-to-all-start.1) | async-done | bytes 524320 | tf_op jit(solution)/shard_map/all_to_all | solution.py:415
  40.5 0.0 copy-done.1
  40.5 5.6 %correlate.1 = (f32[16,32,128]{2,1,0:T(8,128)S(1)}, f32[16,32,128]{2,1,0:T(8,128)S(1)}, f32[16,32,128]{2,1,0:T(8,128)S(1)}, f32[16,32,128]{2,1,0:T(8,128)S(1)}) custom-call(bf16[32,64,128]{2,1,0:T(8,128)(2,1)S(1)} %all-to-all-done.1.src_ref, bf16[64,128,128]{2,1,0:T(8,128)(2,1)} %bitcast.4, bf16[64,128,128]{2,1,0:T(8,128)(2,1)} %bitcast.5, ...), custom_call_target="tpu_custom_call" | custom-call | flops 3000000000 | bytes 6000000 | tf_op jit(solution)/shard_map/correlate/pallas_call | solution.py:350
  46.0 2.8 %collective-permute-start.1 = (f32[16,32,128]{2,1,0:T(8,128)S(1)}, f32[16,32,128]{2,1,0:T(8,128)S(1)}, u32[]{:S(2)}, u32[]{:S(2)}) collective-permute-start(f32[16,32,128]{2,1,0:T(8,128)S(1)} %get-tuple-element.18), channel_id=1, source_target_pairs={{0,32},{32,0},{64,96},{96,64},{1,33},{33,1},{65,97},{97,65},{2,34}... | collective-permute-start | bytes 786440 | tf_op jit(solution)/shard_map/ppermute | solution.py:420
  48.9 0.1 collective-permute-start
  48.9 1.1 %collective-permute-done.1.core_ref = f32[16,32,128]{2,1,0:T(8,128)S(1)} collective-permute-done((f32[16,32,128]{2,1,0:T(8,128)S(1)}, f32[16,32,128]{2,1,0:T(8,128)S(1)}, u32[]{:S(2)}, u32[]{:S(2)}) %collective-permute-start.1) | collective-permute-done | bytes 262176 | tf_op jit(solution)/shard_map/ppermute | solution.py:420
  50.0 2.5 %collective-permute-start.2 = (bf16[16,32,128]{2,1,0:T(8,128)(2,1)S(1)}, bf16[16,32,128]{2,1,0:T(8,128)(2,1)S(1)}, u32[]{:S(2)}, u32[]{:S(2)}) collective-permute-start(bf16[16,32,128]{2,1,0:T(8,128)(2,1)S(1)} %chip_sum.1), channel_id=1, source_target_pairs={{0,64},{32,96},{64,0},{96,32},{1,65},{33,97},{65,1},{97,33},{2,66}... | collective-permute-start | bytes 393224 | tf_op jit(solution)/shard_map/ppermute | solution.py:420
  52.6 0.0 collective-permute-done.core_ref
  52.6 3.8 %collective-permute-done.2.far_ref = bf16[16,32,128]{2,1,0:T(8,128)(2,1)S(1)} collective-permute-done((bf16[16,32,128]{2,1,0:T(8,128)(2,1)S(1)}, bf16[16,32,128]{2,1,0:T(8,128)(2,1)S(1)}, u32[]{:S(2)}, u32[]{:S(2)}) %collective-permute-start.2) | collective-permute-done | bytes 131104 | tf_op jit(solution)/shard_map/ppermute | solution.py:420
  56.3 0.9 %gather_sum.1 = f32[32,16,128]{2,1,0:T(8,128)} custom-call(f32[16,32,128]{2,1,0:T(8,128)S(1)} %get-tuple-element.15.mine_ref, f32[16,32,128]{2,1,0:T(8,128)S(1)} %collective-permute-done.core_ref, bf16[16,32,128]{2,1,0:T(8,128)(2,1)S(1)} %collective-permute-done.2.far_ref), custom_call_target="tpu_custom_call" | custom-call | flops 1000000 | bytes 1000000 | tf_op jit(solution)/shard_map/gather_sum/pallas_call | solution.py:395
  (1 shorter events, 0.0 us)
Async XLA Ops:
  1.9 22.0 %all-to-all-start = ((bf16[32,8,1024]{2,1,0:T(8,128)(2,1)}), bf16[32,8,1024]{2,1,0:T(8,128)(2,1)S(1)}, u32[]{:S(2)}, u32[]{:S(2)}) async-start(bf16[32,8,1024]{2,1,0:T(8,128)(2,1)} %bitcast.3), calls=%async_computation | async-start | bytes 1048576 | tf_op jit(solution)/shard_map/all_to_all | solution.py:412
  12.8 11.1 %copy-start = (bf16[1024,1024]{1,0:T(8,128)(2,1)S(1)}, bf16[1024,1024]{1,0:T(8,128)(2,1)}, u32[]{:S(2)}) copy-start(bf16[1024,1024]{1,0:T(8,128)(2,1)} %constant.4.clone.half_ref.table_ref) | copy-start | bytes 6291460
  25.9 14.6 %all-to-all-start.1 = ((bf16[32,64,128]{2,1,0:T(8,128)(2,1)}), bf16[32,64,128]{2,1,0:T(8,128)(2,1)S(1)}, u32[]{:S(2)}, u32[]{:S(2)}) async-start(bf16[32,64,128]{2,1,0:T(8,128)(2,1)} %source_rows.1), calls=%async_computation.1 | async-start | bytes 1048576 | tf_op jit(solution)/shard_map/all_to_all | solution.py:415
  29.9 10.5 %copy-start.1 = (bf16[2,160,512]{2,1,0:T(8,128)(2,1)S(1)}, bf16[2,160,512]{2,1,0:T(8,128)(2,1)}, u32[]{:S(2)}) copy-start(bf16[2,160,512]{2,1,0:T(8,128)(2,1)} %constant.5.clone.lag_ref) | copy-start | bytes 983044
  46.0 4.0 %collective-permute-start.1 = (f32[16,32,128]{2,1,0:T(8,128)S(1)}, f32[16,32,128]{2,1,0:T(8,128)S(1)}, u32[]{:S(2)}, u32[]{:S(2)}) collective-permute-start(f32[16,32,128]{2,1,0:T(8,128)S(1)} %get-tuple-element.18), channel_id=1, source_target_pairs={{0,32},{32,0},{64,96},{96,64},{1,33},{33,1},{65,97},{97,65},{2,34}... | collective-permute-start | bytes 786440 | tf_op jit(solution)/shard_map/ppermute | solution.py:420
  48.9 3.7 %collective-permute-start = (f32[16,32,128]{2,1,0:T(8,128)S(1)}, f32[16,32,128]{2,1,0:T(8,128)S(1)}, u32[]{:S(2)}, u32[]{:S(2)}) collective-permute-start(f32[16,32,128]{2,1,0:T(8,128)S(1)} %get-tuple-element.16), channel_id=1, source_target_pairs={{0,32},{32,0},{64,96},{96,64},{1,33},{33,1},{65,97},{97,65},{2,34}... | collective-permute-start | bytes 786440 | tf_op jit(solution)/shard_map/ppermute | solution.py:420
  50.0 6.3 %collective-permute-start.2 = (bf16[16,32,128]{2,1,0:T(8,128)(2,1)S(1)}, bf16[16,32,128]{2,1,0:T(8,128)(2,1)S(1)}, u32[]{:S(2)}, u32[]{:S(2)}) collective-permute-start(bf16[16,32,128]{2,1,0:T(8,128)(2,1)S(1)} %chip_sum.1), channel_id=1, source_target_pairs={{0,64},{32,96},{64,0},{96,32},{1,65},{33,97},{65,1},{97,33},{2,66}... | collective-permute-start | bytes 393224 | tf_op jit(solution)/shard_map/ppermute | solution.py:420

commit v7 on v6

--- a/solution.py
+++ b/solution.py
@@ -57,43 +57,66 @@
     return lax.dot_general(a, b, (((1,), (0,)), ((), ())), preferred_element_type=jnp.float32)
 
 
-def pick_body(index_ref, block_ref, raw_ref, out_ref, chan_ref, held_ref, got_ref, zero_ref, sems, out_sems):
+def pick_body(index_ref, block_ref, raw_ref, out_ref, chan_ref, own_ref, held_ref, got_ref, zero_ref, sems, out_sems):
     segs, count, _ = raw_ref.shape
     first = lax.axis_index("ch") * count
+
+    def load(q):
+        start = pl.multiple_of(jnp.clip(chan_ref[q], 0, count - 1) // ROWS * ROWS, ROWS)
+        return pltpu.make_async_copy(raw_ref.at[:, pl.ds(start, ROWS)], held_ref.at[q], sems.at[q])
+
+    def store(q, source):
+        return pltpu.make_async_copy(source, out_ref.at[q], out_sems.at[q])
+
+    zero_ref[...] = jnp.zeros_like(zero_ref)
+    held = jnp.int32(0)
     for s in range(SOURCES):
         rank = jnp.int32(0)
         for t in range(s):
             rank += jnp.where(block_ref[t] == block_ref[s], 1, 0).astype(jnp.int32)
-        chan_ref[block_ref[s] * PER_BLOCK + rank] = index_ref[s] - first
-
-    def ours(q):
-        return (chan_ref[q] >= 0) & (chan_ref[q] < count)
-
-    def load(q):
-        start = pl.multiple_of(jnp.clip(chan_ref[q], 0, count - 1) // ROWS * ROWS, ROWS)
-        return pltpu.make_async_copy(raw_ref.at[:, pl.ds(start, ROWS)], held_ref.at[q], sems.at[q])
-
-    def store(q, source):
-        return pltpu.make_async_copy(source, out_ref.at[q], out_sems.at[q])
-
-    for q in range(SOURCES):
-        pl.when(ours(q))(lambda q=q: load(q).start())
-    zero_ref[...] = jnp.zeros_like(zero_ref)
-    for q in range(SOURCES):
-        pl.when(jnp.logical_not(ours(q)))(lambda q=q: store(q, zero_ref).start())
+        q = block_ref[s] * PER_BLOCK + rank
+        chan = index_ref[s] - first
+        chan_ref[q] = chan
+        ours = (chan >= 0) & (chan < count)
+        own_ref[held] = q
+        held += jnp.where(ours, 1, 0).astype(jnp.int32)
+
+        @pl.when(ours)
+        def _(q=q):
+            load(q).start()
+
+        @pl.when(jnp.logical_not(ours))
+        def _(q=q):
+            store(q, zero_ref).start()
+
     row = lax.broadcasted_iota(jnp.int32, (segs, segs * ROWS), 0)
     column = lax.broadcasted_iota(jnp.int32, (segs, segs * ROWS), 1)
-    for q in range(SOURCES):
-
-        @pl.when(ours(q))
-        def _(q=q):
-            load(q).wait()
+
+    def two(i, carry):
+        qs = (own_ref[2 * i], own_ref[jnp.minimum(2 * i + 1, held - 1)])
+        more = 2 * i + 1 < held
+        load(qs[0]).wait()
+
+        @pl.when(more)
+        def _():
+            load(qs[1]).wait()
+
+        gots = []
+        for q in qs:
             hit = column == row * ROWS + chan_ref[q] % ROWS
             rows = held_ref[q].reshape(segs * ROWS, SEGLEN)
-            got = nn_dot(jnp.where(hit, 1.0, 0.0).astype(jnp.bfloat16), rows)
-            got_ref[q] = got.astype(jnp.bfloat16).reshape(segs // 8, 8, SEGLEN)
-            store(q, got_ref.at[q]).start()
-
+            gots.append(nn_dot(jnp.where(hit, 1.0, 0.0).astype(jnp.bfloat16), rows))
+        for k, got in enumerate(gots):
+            got_ref[2 * i + k] = got.astype(jnp.bfloat16).reshape(segs // 8, 8, SEGLEN)
+        store(qs[0], got_ref.at[2 * i]).start()
+
+        @pl.when(more)
+        def _():
+            store(qs[1], got_ref.at[2 * i + 1]).start()
+
+        return carry
+
+    lax.fori_loop(0, (held + 1) // 2, two, 0)
     for q in range(SOURCES):
         store(q, zero_ref).wait()
 
@@ -109,6 +132,7 @@
             in_specs=[pl.BlockSpec(memory_space=pl.ANY)],
             out_specs=pl.BlockSpec(memory_space=pl.ANY),
             scratch_shapes=[
+                pltpu.SMEM((SOURCES,), jnp.int32),
                 pltpu.SMEM((SOURCES,), jnp.int32),
                 pltpu.VMEM((SOURCES, segs, ROWS, length), raw.dtype),
                 pltpu.VMEM((SOURCES, *shape), raw.dtype),
@@ -124,7 +148,7 @@
     )(source_index, source_block, raw)
 
 
-def source_body(parts_ref, table_ref, after_ref, out_ref):
+def source_body(parts_ref, table_ref, after_ref, out_ref, tile_ref, sems):
     total = jnp.sum(parts_ref[...].astype(jnp.float32), axis=0)
     spectrum = nt_dot(total.astype(jnp.bfloat16), table_ref[...])
     real = spectrum[:, :FREQS]
@@ -161,7 +185,14 @@
         rows.append(jnp.where(lane < 64, re, pltpu.roll(im, 64, 1)))
         rows.append(jnp.where(lane < 64, pltpu.roll(re, 64, 1), im))
     packed = jnp.concatenate(rows, axis=0).astype(jnp.bfloat16)
-    out_ref[...] = jnp.broadcast_to(packed[None], out_ref.shape)
+    tile_ref[...] = jnp.broadcast_to(packed[None], tile_ref.shape)
+    size = tile_ref.shape[0]
+    copies = []
+    for i in range(out_ref.shape[0] // size):
+        copies.append(pltpu.make_async_copy(tile_ref, out_ref.at[pl.ds(i * size, size)], sems.at[i]))
+        copies[-1].start()
+    for copy in copies:
+        copy.wait()
 
 
 def source_rows(parts, table, after):
@@ -169,7 +200,11 @@
         source_body,
         out_shape=jax.ShapeDtypeStruct((parts.shape[0], GROUPS, 128), jnp.bfloat16),
         in_specs=[pl.BlockSpec(memory_space=pltpu.VMEM)] * 2 + [pl.BlockSpec(memory_space=pl.ANY)],
-        out_specs=pl.BlockSpec(memory_space=pltpu.VMEM),
+        out_specs=pl.BlockSpec(memory_space=pl.ANY),
+        scratch_shapes=[
+            pltpu.VMEM((parts.shape[0] // 4, GROUPS, 128), jnp.bfloat16),
+            pltpu.SemaphoreType.DMA((4,)),
+        ],
         compiler_params=pltpu.CompilerParams(vmem_limit_bytes=SOURCE_VMEM),
         cost_estimate=pl.CostEstimate(flops=2 * 8 * 1024 * 1024, bytes_accessed=3 * 10**6, transcendentals=0),
         name="source_rows",

time: 57.7 us -> 57.7 us (level)
  Pallas kernels: 25 us -> 26.2 us
  starting transfers between devices: 20.4 us -> 19.3 us
    pallas_call x1, Pallas kernels: 1.92 us -> 3.05 us  [pick(): pl.pallas_call(pick_body, grid_spec=pltpu.PrefetchScalarGridSpec(num_scal...]
    all_to_all x1, starting transfers between devices: 10.9 us -> 9.8 us  [local(): parts = lax.all_to_all(picked.reshape(ways, 8, SEGLEN), 'ch', 0, 0)]
where the time goes in v7:
time: 57.7 us; the launch traced here: 57.3 us
  Pallas kernels  26.2 us (45%)
  starting transfers between devices  19.3 us (33%)
  waiting for transfers between devices  11.7 us (20%)
    pallas_call x2, Pallas kernels, whiten(): pl.pallas_call(whiten_body, grid=(pairs,), in_specs=[pl.BlockSpec((2, cou...  14.7 us
    all_to_all x1, starting transfers between devices, local(): parts = lax.all_to_all(picked.reshape(ways, 8, SEGLEN), 'ch', 0, 0)  9.8 us
    pallas_call x1, Pallas kernels, correlate(): pl.pallas_call(correlate_body, in_specs=[vmem, anywhere, anywhere, anywhe...  5.57 us
    ppermute x3, starting transfers between devices, swap(): return lax.ppermute(x, 'seg', [(i, i ^ r) for i in range(4)])  5.42 us
    ppermute x3, waiting for transfers between devices, swap(): return lax.ppermute(x, 'seg', [(i, i ^ r) for i in range(4)])  4.84 us
    all_to_all x1, starting transfers between devices, local(): src = lax.all_to_all(spread, 'ch', 0, 0)  4.07 us
    all_to_all x1, waiting for transfers between devices, local(): parts = lax.all_to_all(picked.reshape(ways, 8, SEGLEN), 'ch', 0, 0)  3.67 us
    all_to_all x1, waiting for transfers between devices, local(): src = lax.all_to_all(spread, 'ch', 0, 0)  3.22 us
  transfers between devices with their start and end apart: 5, of which 4 were waited for; matrix products, arithmetic and copies ran while one was open for 0% of the time, Pallas kernels for 26%

profile of v7, /device:TPU:1, one launch (start us, length us, event | category | flops | bytes accessed | tf_op | source)
XLA Modules:
  0.0 57.3 jit_solution(14747972308700059469)
XLA Ops:
  0.0 3.0 %pick.1 = bf16[16,2,8,1024]{3,2,1,0:T(8,128)(2,1)} custom-call(s32[16]{0:T(128)} %index_ref.1, s32[16]{0:T(128)} %block_ref.1, bf16[16,128,1024]{2,1,0:T(8,128)(2,1)} %raw_ref.5), custom_call_target="tpu_custom_call" | custom-call | flops 100000000 | bytes 3000000 | tf_op jit(solution)/shard_map/pick/pallas_call | solution.py:127
  3.1 9.8 %all-to-all-start = ((bf16[32,8,1024]{2,1,0:T(8,128)(2,1)}), bf16[32,8,1024]{2,1,0:T(8,128)(2,1)S(1)}, u32[]{:S(2)}, u32[]{:S(2)}) async-start(bf16[32,8,1024]{2,1,0:T(8,128)(2,1)} %bitcast.3), calls=%async_computation | async-start | bytes 1048576 | tf_op jit(solution)/shard_map/all_to_all | solution.py:447
  12.9 0.0 copy-start
  12.9 7.4 %whiten0.1 = (bf16[64,2,4,16,128]{4,3,2,1,0:T(8,128)(2,1)}, f32[8,128]{1,0:T(8,128)S(1)}) custom-call(bf16[16,128,1024]{2,1,0:T(8,128)(2,1)} %raw_ref.5, bf16[1024,1024]{1,0:T(8,128)(2,1)} %constant.4.clone.half_ref.table_ref), custom_call_target="tpu_custom_call" | custom-call | flops 2147483648 | bytes 6000000 | tf_op jit(solution)/shard_map/whiten0/pallas_call | solution.py:256
  20.3 3.7 %all-to-all-done.parts_ref = bf16[32,8,1024]{2,1,0:T(8,128)(2,1)S(1)} async-done(((bf16[32,8,1024]{2,1,0:T(8,128)(2,1)}), bf16[32,8,1024]{2,1,0:T(8,128)(2,1)S(1)}, u32[]{:S(2)}, u32[]{:S(2)}) %all-to-all-start) | async-done | bytes 524320 | tf_op jit(solution)/shard_map/all_to_all | solution.py:447
  24.0 0.0 copy-done
  24.0 1.9 %source_rows.1 = bf16[32,64,128]{2,1,0:T(8,128)(2,1)} custom-call(bf16[32,8,1024]{2,1,0:T(8,128)(2,1)S(1)} %all-to-all-done.parts_ref, bf16[1024,1024]{1,0:T(8,128)(2,1)S(1)} %copy-done, f32[8,128]{1,0:T(8,128)S(1)} %get-tuple-element.12.after_ref), custom_call_target="tpu_custom_call" | custom-call | flops 16777216 | bytes 3000000 | tf_op jit(solution)/shard_map/source_rows/pallas_call | solution.py:199
  25.9 4.1 %all-to-all-start.1 = ((bf16[32,64,128]{2,1,0:T(8,128)(2,1)}), bf16[32,64,128]{2,1,0:T(8,128)(2,1)S(1)}, u32[]{:S(2)}, u32[]{:S(2)}) async-start(bf16[32,64,128]{2,1,0:T(8,128)(2,1)} %source_rows.1), calls=%async_computation.1 | async-start | bytes 1048576 | tf_op jit(solution)/shard_map/all_to_all | solution.py:450
  30.0 0.0 copy-start.1
  30.0 7.3 %whiten1.1 = (bf16[64,2,4,16,128]{4,3,2,1,0:T(8,128)(2,1)}, f32[8,128]{1,0:T(8,128)}) custom-call(bf16[16,128,1024]{2,1,0:T(8,128)(2,1)} %raw_ref.5, bf16[1024,1024]{1,0:T(8,128)(2,1)} %constant.4.clone.half_ref.table_ref), custom_call_target="tpu_custom_call" | custom-call | flops 2147483648 | bytes 6000000 | tf_op jit(solution)/shard_map/whiten1/pallas_call | solution.py:256
  37.3 3.2 %all-to-all-done.1.src_ref = bf16[32,64,128]{2,1,0:T(8,128)(2,1)S(1)} async-done(((bf16[32,64,128]{2,1,0:T(8,128)(2,1)}), bf16[32,64,128]{2,1,0:T(8,128)(2,1)S(1)}, u32[]{:S(2)}, u32[]{:S(2)}) %all-to-all-start.1) | async-done | bytes 524320 | tf_op jit(solution)/shard_map/all_to_all | solution.py:450
  40.5 0.0 copy-done.1
  40.5 5.6 %correlate.1 = (f32[16,32,128]{2,1,0:T(8,128)S(1)}, f32[16,32,128]{2,1,0:T(8,128)S(1)}, f32[16,32,128]{2,1,0:T(8,128)S(1)}, f32[16,32,128]{2,1,0:T(8,128)S(1)}) custom-call(bf16[32,64,128]{2,1,0:T(8,128)(2,1)S(1)} %all-to-all-done.1.src_ref, bf16[64,128,128]{2,1,0:T(8,128)(2,1)} %bitcast.4, bf16[64,128,128]{2,1,0:T(8,128)(2,1)} %bitcast.5, ...), custom_call_target="tpu_custom_call" | custom-call | flops 3000000000 | bytes 6000000 | tf_op jit(solution)/shard_map/correlate/pallas_call | solution.py:385
  46.1 2.8 %collective-permute-start.1 = (f32[16,32,128]{2,1,0:T(8,128)S(1)}, f32[16,32,128]{2,1,0:T(8,128)S(1)}, u32[]{:S(2)}, u32[]{:S(2)}) collective-permute-start(f32[16,32,128]{2,1,0:T(8,128)S(1)} %get-tuple-element.18), channel_id=1, source_target_pairs={{0,32},{32,0},{64,96},{96,64},{1,33},{33,1},{65,97},{97,65},{2,34}... | collective-permute-start | bytes 786440 | tf_op jit(solution)/shard_map/ppermute | solution.py:455
  48.9 0.1 collective-permute-start
  49.0 1.1 %collective-permute-done.1.core_ref = f32[16,32,128]{2,1,0:T(8,128)S(1)} collective-permute-done((f32[16,32,128]{2,1,0:T(8,128)S(1)}, f32[16,32,128]{2,1,0:T(8,128)S(1)}, u32[]{:S(2)}, u32[]{:S(2)}) %collective-permute-start.1) | collective-permute-done | bytes 262176 | tf_op jit(solution)/shard_map/ppermute | solution.py:455
  50.1 2.5 %collective-permute-start.2 = (bf16[16,32,128]{2,1,0:T(8,128)(2,1)S(1)}, bf16[16,32,128]{2,1,0:T(8,128)(2,1)S(1)}, u32[]{:S(2)}, u32[]{:S(2)}) collective-permute-start(bf16[16,32,128]{2,1,0:T(8,128)(2,1)S(1)} %chip_sum.1), channel_id=1, source_target_pairs={{0,64},{32,96},{64,0},{96,32},{1,65},{33,97},{65,1},{97,33},{2,66}... | collective-permute-start | bytes 393224 | tf_op jit(solution)/shard_map/ppermute | solution.py:455
  52.6 0.0 collective-permute-done.core_ref
  52.6 3.8 %collective-permute-done.2.far_ref = bf16[16,32,128]{2,1,0:T(8,128)(2,1)S(1)} collective-permute-done((bf16[16,32,128]{2,1,0:T(8,128)(2,1)S(1)}, bf16[16,32,128]{2,1,0:T(8,128)(2,1)S(1)}, u32[]{:S(2)}, u32[]{:S(2)}) %collective-permute-start.2) | collective-permute-done | bytes 131104 | tf_op jit(solution)/shard_map/ppermute | solution.py:455
  56.4 0.9 %gather_sum.1 = f32[32,16,128]{2,1,0:T(8,128)} custom-call(f32[16,32,128]{2,1,0:T(8,128)S(1)} %get-tuple-element.15.mine_ref, f32[16,32,128]{2,1,0:T(8,128)S(1)} %collective-permute-done.core_ref, bf16[16,32,128]{2,1,0:T(8,128)(2,1)S(1)} %collective-permute-done.2.far_ref), custom_call_target="tpu_custom_call" | custom-call | flops 1000000 | bytes 1000000 | tf_op jit(solution)/shard_map/gather_sum/pallas_call | solution.py:430
  (1 shorter events, 0.0 us)
Async XLA Ops:
  3.1 20.9 %all-to-all-start = ((bf16[32,8,1024]{2,1,0:T(8,128)(2,1)}), bf16[32,8,1024]{2,1,0:T(8,128)(2,1)S(1)}, u32[]{:S(2)}, u32[]{:S(2)}) async-start(bf16[32,8,1024]{2,1,0:T(8,128)(2,1)} %bitcast.3), calls=%async_computation | async-start | bytes 1048576 | tf_op jit(solution)/shard_map/all_to_all | solution.py:447
  12.9 11.1 %copy-start = (bf16[1024,1024]{1,0:T(8,128)(2,1)S(1)}, bf16[1024,1024]{1,0:T(8,128)(2,1)}, u32[]{:S(2)}) copy-start(bf16[1024,1024]{1,0:T(8,128)(2,1)} %constant.4.clone.half_ref.table_ref) | copy-start | bytes 6291460
  25.9 14.6 %all-to-all-start.1 = ((bf16[32,64,128]{2,1,0:T(8,128)(2,1)}), bf16[32,64,128]{2,1,0:T(8,128)(2,1)S(1)}, u32[]{:S(2)}, u32[]{:S(2)}) async-start(bf16[32,64,128]{2,1,0:T(8,128)(2,1)} %source_rows.1), calls=%async_computation.1 | async-start | bytes 1048576 | tf_op jit(solution)/shard_map/all_to_all | solution.py:450
  30.0 10.5 %copy-start.1 = (bf16[2,160,512]{2,1,0:T(8,128)(2,1)S(1)}, bf16[2,160,512]{2,1,0:T(8,128)(2,1)}, u32[]{:S(2)}) copy-start(bf16[2,160,512]{2,1,0:T(8,128)(2,1)} %constant.5.clone.lag_ref) | copy-start | bytes 983044
  46.1 4.0 %collective-permute-start.1 = (f32[16,32,128]{2,1,0:T(8,128)S(1)}, f32[16,32,128]{2,1,0:T(8,128)S(1)}, u32[]{:S(2)}, u32[]{:S(2)}) collective-permute-start(f32[16,32,128]{2,1,0:T(8,128)S(1)} %get-tuple-element.18), channel_id=1, source_target_pairs={{0,32},{32,0},{64,96},{96,64},{1,33},{33,1},{65,97},{97,65},{2,34}... | collective-permute-start | bytes 786440 | tf_op jit(solution)/shard_map/ppermute | solution.py:455
  48.9 3.7 %collective-permute-start = (f32[16,32,128]{2,1,0:T(8,128)S(1)}, f32[16,32,128]{2,1,0:T(8,128)S(1)}, u32[]{:S(2)}, u32[]{:S(2)}) collective-permute-start(f32[16,32,128]{2,1,0:T(8,128)S(1)} %get-tuple-element.16), channel_id=1, source_target_pairs={{0,32},{32,0},{64,96},{96,64},{1,33},{33,1},{65,97},{97,65},{2,34}... | collective-permute-start | bytes 786440 | tf_op jit(solution)/shard_map/ppermute | solution.py:455
  50.1 6.3 %collective-permute-start.2 = (bf16[16,32,128]{2,1,0:T(8,128)(2,1)S(1)}, bf16[16,32,128]{2,1,0:T(8,128)(2,1)S(1)}, u32[]{:S(2)}, u32[]{:S(2)}) collective-permute-start(bf16[16,32,128]{2,1,0:T(8,128)(2,1)S(1)} %chip_sum.1), channel_id=1, source_target_pairs={{0,64},{32,96},{64,0},{96,32},{1,65},{33,97},{65,1},{97,33},{2,66}... | collective-permute-start | bytes 393224 | tf_op jit(solution)/shard_map/ppermute | solution.py:455

commit v8 on v6

--- a/solution.py
+++ b/solution.py
@@ -186,7 +186,7 @@
 
     count = raw_ref.shape[1]
     width = 2 * count
-    step = 32
+    step = 16
     size = step + 16
     zero = jnp.zeros((8, width), jnp.float32)
     amp_ref[0:8, :] = zero

time: 57.7 us -> 57.9 us (level)
  no operation moved by 1% of the time
where the time goes in v8:
time: 57.9 us; the launch traced here: 57.5 us
  Pallas kernels  25.3 us (44%)
  starting transfers between devices  20.6 us (36%)
  waiting for transfers between devices  11.5 us (20%)
    pallas_call x2, Pallas kernels, whiten(): pl.pallas_call(whiten_body, grid=(pairs,), in_specs=[pl.BlockSpec((2, cou...  14.9 us
    all_to_all x1, starting transfers between devices, local(): parts = lax.all_to_all(picked.reshape(ways, 8, SEGLEN), 'ch', 0, 0)  11 us
    pallas_call x1, Pallas kernels, correlate(): pl.pallas_call(correlate_body, in_specs=[vmem, anywhere, anywhere, anywhe...  5.57 us
    ppermute x3, starting transfers between devices, swap(): return lax.ppermute(x, 'seg', [(i, i ^ r) for i in range(4)])  5.39 us
    ppermute x3, waiting for transfers between devices, swap(): return lax.ppermute(x, 'seg', [(i, i ^ r) for i in range(4)])  4.83 us
    all_to_all x1, starting transfers between devices, local(): src = lax.all_to_all(spread, 'ch', 0, 0)  4.16 us
    all_to_all x1, waiting for transfers between devices, local(): parts = lax.all_to_all(picked.reshape(ways, 8, SEGLEN), 'ch', 0, 0)  3.57 us
    all_to_all x1, waiting for transfers between devices, local(): src = lax.all_to_all(spread, 'ch', 0, 0)  3.15 us
  transfers between devices with their start and end apart: 5, of which 4 were waited for; matrix products, arithmetic and copies ran while one was open for 0% of the time, Pallas kernels for 26%

profile of v8, /device:TPU:1, one launch (start us, length us, event | category | flops | bytes accessed | tf_op | source)
XLA Modules:
  0.0 57.5 jit_solution(4004329569013508619)
XLA Ops:
  0.0 1.9 %pick.1 = bf16[16,2,8,1024]{3,2,1,0:T(8,128)(2,1)} custom-call(s32[16]{0:T(128)} %index_ref.1, s32[16]{0:T(128)} %block_ref.1, bf16[16,128,1024]{2,1,0:T(8,128)(2,1)} %raw_ref.5), custom_call_target="tpu_custom_call" | custom-call | flops 100000000 | bytes 3000000 | tf_op jit(solution)/shard_map/pick/pallas_call | solution.py:104
  1.9 11.0 %all-to-all-start = ((bf16[32,8,1024]{2,1,0:T(8,128)(2,1)}), bf16[32,8,1024]{2,1,0:T(8,128)(2,1)S(1)}, u32[]{:S(2)}, u32[]{:S(2)}) async-start(bf16[32,8,1024]{2,1,0:T(8,128)(2,1)} %bitcast.3), calls=%async_computation | async-start | bytes 1048576 | tf_op jit(solution)/shard_map/all_to_all | solution.py:412
  13.0 0.0 copy-start
  13.0 7.5 %whiten0.1 = (bf16[64,2,4,16,128]{4,3,2,1,0:T(8,128)(2,1)}, f32[8,128]{1,0:T(8,128)S(1)}) custom-call(bf16[16,128,1024]{2,1,0:T(8,128)(2,1)} %raw_ref.5, bf16[1024,1024]{1,0:T(8,128)(2,1)} %constant.4.clone.half_ref.table_ref), custom_call_target="tpu_custom_call" | custom-call | flops 2147483648 | bytes 6000000 | tf_op jit(solution)/shard_map/whiten0/pallas_call | solution.py:221
  20.5 3.6 %all-to-all-done.parts_ref = bf16[32,8,1024]{2,1,0:T(8,128)(2,1)S(1)} async-done(((bf16[32,8,1024]{2,1,0:T(8,128)(2,1)}), bf16[32,8,1024]{2,1,0:T(8,128)(2,1)S(1)}, u32[]{:S(2)}, u32[]{:S(2)}) %all-to-all-start) | async-done | bytes 524320 | tf_op jit(solution)/shard_map/all_to_all | solution.py:412
  24.1 0.0 copy-done
  24.1 1.9 %source_rows.1 = bf16[32,64,128]{2,1,0:T(8,128)(2,1)} custom-call(bf16[32,8,1024]{2,1,0:T(8,128)(2,1)S(1)} %all-to-all-done.parts_ref, bf16[1024,1024]{1,0:T(8,128)(2,1)S(1)} %copy-done, f32[8,128]{1,0:T(8,128)S(1)} %get-tuple-element.12.after_ref), custom_call_target="tpu_custom_call" | custom-call | flops 16777216 | bytes 3000000 | tf_op jit(solution)/shard_map/source_rows/pallas_call | solution.py:168
  26.0 4.2 %all-to-all-start.1 = ((bf16[32,64,128]{2,1,0:T(8,128)(2,1)}), bf16[32,64,128]{2,1,0:T(8,128)(2,1)S(1)}, u32[]{:S(2)}, u32[]{:S(2)}) async-start(bf16[32,64,128]{2,1,0:T(8,128)(2,1)} %source_rows.1), calls=%async_computation.1 | async-start | bytes 1048576 | tf_op jit(solution)/shard_map/all_to_all | solution.py:415
  30.2 0.0 copy-start.1
  30.2 7.4 %whiten1.1 = (bf16[64,2,4,16,128]{4,3,2,1,0:T(8,128)(2,1)}, f32[8,128]{1,0:T(8,128)}) custom-call(bf16[16,128,1024]{2,1,0:T(8,128)(2,1)} %raw_ref.5, bf16[1024,1024]{1,0:T(8,128)(2,1)} %constant.4.clone.half_ref.table_ref), custom_call_target="tpu_custom_call" | custom-call | flops 2147483648 | bytes 6000000 | tf_op jit(solution)/shard_map/whiten1/pallas_call | solution.py:221
  37.6 3.2 %all-to-all-done.1.src_ref = bf16[32,64,128]{2,1,0:T(8,128)(2,1)S(1)} async-done(((bf16[32,64,128]{2,1,0:T(8,128)(2,1)}), bf16[32,64,128]{2,1,0:T(8,128)(2,1)S(1)}, u32[]{:S(2)}, u32[]{:S(2)}) %all-to-all-start.1) | async-done | bytes 524320 | tf_op jit(solution)/shard_map/all_to_all | solution.py:415
  40.8 0.0 copy-done.1
  40.8 5.6 %correlate.1 = (f32[16,32,128]{2,1,0:T(8,128)S(1)}, f32[16,32,128]{2,1,0:T(8,128)S(1)}, f32[16,32,128]{2,1,0:T(8,128)S(1)}, f32[16,32,128]{2,1,0:T(8,128)S(1)}) custom-call(bf16[32,64,128]{2,1,0:T(8,128)(2,1)S(1)} %all-to-all-done.1.src_ref, bf16[64,128,128]{2,1,0:T(8,128)(2,1)} %bitcast.4, bf16[64,128,128]{2,1,0:T(8,128)(2,1)} %bitcast.5, ...), custom_call_target="tpu_custom_call" | custom-call | flops 3000000000 | bytes 6000000 | tf_op jit(solution)/shard_map/correlate/pallas_call | solution.py:350
  46.4 2.8 %collective-permute-start.1 = (f32[16,32,128]{2,1,0:T(8,128)S(1)}, f32[16,32,128]{2,1,0:T(8,128)S(1)}, u32[]{:S(2)}, u32[]{:S(2)}) collective-permute-start(f32[16,32,128]{2,1,0:T(8,128)S(1)} %get-tuple-element.18), channel_id=1, source_target_pairs={{0,32},{32,0},{64,96},{96,64},{1,33},{33,1},{65,97},{97,65},{2,34}... | collective-permute-start | bytes 786440 | tf_op jit(solution)/shard_map/ppermute | solution.py:420
  49.1 0.1 collective-permute-start
  49.2 1.1 %collective-permute-done.1.core_ref = f32[16,32,128]{2,1,0:T(8,128)S(1)} collective-permute-done((f32[16,32,128]{2,1,0:T(8,128)S(1)}, f32[16,32,128]{2,1,0:T(8,128)S(1)}, u32[]{:S(2)}, u32[]{:S(2)}) %collective-permute-start.1) | collective-permute-done | bytes 262176 | tf_op jit(solution)/shard_map/ppermute | solution.py:420
  50.3 2.5 %collective-permute-start.2 = (bf16[16,32,128]{2,1,0:T(8,128)(2,1)S(1)}, bf16[16,32,128]{2,1,0:T(8,128)(2,1)S(1)}, u32[]{:S(2)}, u32[]{:S(2)}) collective-permute-start(bf16[16,32,128]{2,1,0:T(8,128)(2,1)S(1)} %chip_sum.1), channel_id=1, source_target_pairs={{0,64},{32,96},{64,0},{96,32},{1,65},{33,97},{65,1},{97,33},{2,66}... | collective-permute-start | bytes 393224 | tf_op jit(solution)/shard_map/ppermute | solution.py:420
  52.8 0.0 collective-permute-done.core_ref
  52.8 3.8 %collective-permute-done.2.far_ref = bf16[16,32,128]{2,1,0:T(8,128)(2,1)S(1)} collective-permute-done((bf16[16,32,128]{2,1,0:T(8,128)(2,1)S(1)}, bf16[16,32,128]{2,1,0:T(8,128)(2,1)S(1)}, u32[]{:S(2)}, u32[]{:S(2)}) %collective-permute-start.2) | collective-permute-done | bytes 131104 | tf_op jit(solution)/shard_map/ppermute | solution.py:420
  56.6 0.9 %gather_sum.1 = f32[32,16,128]{2,1,0:T(8,128)} custom-call(f32[16,32,128]{2,1,0:T(8,128)S(1)} %get-tuple-element.15.mine_ref, f32[16,32,128]{2,1,0:T(8,128)S(1)} %collective-permute-done.core_ref, bf16[16,32,128]{2,1,0:T(8,128)(2,1)S(1)} %collective-permute-done.2.far_ref), custom_call_target="tpu_custom_call" | custom-call | flops 1000000 | bytes 1000000 | tf_op jit(solution)/shard_map/gather_sum/pallas_call | solution.py:395
  (1 shorter events, 0.0 us)
Async XLA Ops:
  1.9 22.2 %all-to-all-start = ((bf16[32,8,1024]{2,1,0:T(8,128)(2,1)}), bf16[32,8,1024]{2,1,0:T(8,128)(2,1)S(1)}, u32[]{:S(2)}, u32[]{:S(2)}) async-start(bf16[32,8,1024]{2,1,0:T(8,128)(2,1)} %bitcast.3), calls=%async_computation | async-start | bytes 1048576 | tf_op jit(solution)/shard_map/all_to_all | solution.py:412
  13.0 11.1 %copy-start = (bf16[1024,1024]{1,0:T(8,128)(2,1)S(1)}, bf16[1024,1024]{1,0:T(8,128)(2,1)}, u32[]{:S(2)}) copy-start(bf16[1024,1024]{1,0:T(8,128)(2,1)} %constant.4.clone.half_ref.table_ref) | copy-start | bytes 6291460
  26.0 14.7 %all-to-all-start.1 = ((bf16[32,64,128]{2,1,0:T(8,128)(2,1)}), bf16[32,64,128]{2,1,0:T(8,128)(2,1)S(1)}, u32[]{:S(2)}, u32[]{:S(2)}) async-start(bf16[32,64,128]{2,1,0:T(8,128)(2,1)} %source_rows.1), calls=%async_computation.1 | async-start | bytes 1048576 | tf_op jit(solution)/shard_map/all_to_all | solution.py:415
  30.2 10.6 %copy-start.1 = (bf16[2,160,512]{2,1,0:T(8,128)(2,1)S(1)}, bf16[2,160,512]{2,1,0:T(8,128)(2,1)}, u32[]{:S(2)}) copy-start(bf16[2,160,512]{2,1,0:T(8,128)(2,1)} %constant.5.clone.lag_ref) | copy-start | bytes 983044
  46.4 3.9 %collective-permute-start.1 = (f32[16,32,128]{2,1,0:T(8,128)S(1)}, f32[16,32,128]{2,1,0:T(8,128)S(1)}, u32[]{:S(2)}, u32[]{:S(2)}) collective-permute-start(f32[16,32,128]{2,1,0:T(8,128)S(1)} %get-tuple-element.18), channel_id=1, source_target_pairs={{0,32},{32,0},{64,96},{96,64},{1,33},{33,1},{65,97},{97,65},{2,34}... | collective-permute-start | bytes 786440 | tf_op jit(solution)/shard_map/ppermute | solution.py:420
  49.1 3.7 %collective-permute-start = (f32[16,32,128]{2,1,0:T(8,128)S(1)}, f32[16,32,128]{2,1,0:T(8,128)S(1)}, u32[]{:S(2)}, u32[]{:S(2)}) collective-permute-start(f32[16,32,128]{2,1,0:T(8,128)S(1)} %get-tuple-element.16), channel_id=1, source_target_pairs={{0,32},{32,0},{64,96},{96,64},{1,33},{33,1},{65,97},{97,65},{2,34}... | collective-permute-start | bytes 786440 | tf_op jit(solution)/shard_map/ppermute | solution.py:420
  50.3 6.3 %collective-permute-start.2 = (bf16[16,32,128]{2,1,0:T(8,128)(2,1)S(1)}, bf16[16,32,128]{2,1,0:T(8,128)(2,1)S(1)}, u32[]{:S(2)}, u32[]{:S(2)}) collective-permute-start(bf16[16,32,128]{2,1,0:T(8,128)(2,1)S(1)} %chip_sum.1), channel_id=1, source_target_pairs={{0,64},{32,96},{64,0},{96,32},{1,65},{33,97},{65,1},{97,33},{2,66}... | collective-permute-start | bytes 393224 | tf_op jit(solution)/shard_map/ppermute | solution.py:420
